TPU v7x, 128 devices: a whole 4x4x4 slice. The times are simulated.
128 devices in a mesh: pre: 4 (over x), head: 8 (over y, core), cache: 4 (over z).
Axes of the slice: x: 4, y: 4, z: 4, core: 2. Of those that a mesh axis runs over, the one named last changes fastest.
Arguments:
- prompt_kv: bfloat16 [16, 8, 128, 128, 256], P('cache', 'head', 'pre'), may hold values from -12 to 12
- kept: int32 [16, 8, 4, 8], P('cache', 'head', 'pre'), may hold values from 0 to 31, as said below
- live_count: int32 [16, 8], P('cache', 'head'), may hold values from 1 to 8, as said below
- queries: bfloat16 [3, 4, 4, 8192], P(None, None, 'pre', 'head'), may hold values from -8 to 8
- out_weight: bfloat16 [8192, 8, 4, 256], P('head', None, 'cache'), may hold values from -0.25 to 0.25
- prefill_x: bfloat16 [8192, 8192], P(('pre', 'cache')), may hold values from -6 to 6
- prefill_gain: bfloat16 [8192], replicated, may hold values from 0.099609375 to 1.8984375
- kv_weight: bfloat16 [8192, 8, 256], P(None, 'head'), may hold values from -0.0625 to 0.0625
Outputs:
- attended: bfloat16 [3, 4, 4, 8192], P(None, None, 'pre', ('head', 'cache'))
- next_kv: bfloat16 [8192, 8, 256], P(('pre', 'cache'), 'head')
Inputs may be any that keep to these rules, and one draw needn't show every extreme that they name: `kept`: within one request, KV head and section the 8 block numbers are distinct. The first live_count entries of each section's list are live; every draw has a head with all 8 entries live.
All inputs are finite; a program needn't handle non-finite values.
Results may differ from a plain program's by a relative error of at most 0.02.
Values may be sent and summed in bfloat16 or wider, within the bound.
No kernel may reach another device: no remote copies, remote signals or barrier semaphores. Data moves between devices by JAX's collectives and lax.ppermute only.
A program may use at most 128 MiB of HBM per device.

v0:
```python
import math

import jax
import jax.numpy as jnp
from jax import lax
from jax.sharding import PartitionSpec as P


def combined_all(part, axis, combine):
    gathered = jax.tree.map(lambda a: lax.all_gather(a, axis), part)

    def take(source):
        return jax.tree.map(lambda a: lax.dynamic_index_in_dim(a, source, 0, False), gathered)

    return lax.fori_loop(
        1, lax.axis_size(axis), lambda source, state: combine(state, take(source)), take(0)
    )


def combine_parts(earlier, latter):
    maxima = jnp.maximum(earlier[0], latter[0])
    scale_one = jnp.exp(earlier[0] - maxima)
    scale_two = jnp.exp(latter[0] - maxima)
    totals = earlier[1] * scale_one + latter[1] * scale_two
    weighted = earlier[2] * scale_one[..., None] + latter[2] * scale_two[..., None]
    return (maxima, totals, weighted)


def partial_softmax(query_rows, key_rows, values, tok_mask):
    factor = 1.0 / math.sqrt(query_rows.shape[-1])
    scores = (
        jnp.einsum("srhgd,rhtd->srhgt", query_rows, key_rows, preferred_element_type=jnp.float32)
        * factor
    )
    scores = jnp.where(tok_mask[None, :, :, None, :], scores, jnp.float32(-1e30))
    maxima = jnp.max(scores, axis=-1)
    exp_terms = jnp.exp(scores - maxima[..., None])
    totals = jnp.sum(exp_terms, axis=-1)
    weighted = jnp.einsum(
        "srhgt,rhtd->srhgd",
        exp_terms.astype(jnp.bfloat16),
        values,
        preferred_element_type=jnp.float32,
    )
    return (maxima, totals, weighted)


def body(prompt_kv, kept, live_count, queries, out_weight, prefill_x, prefill_gain, kv_weight):
    rows_group = prompt_kv.shape[0]
    heads_local = prompt_kv.shape[1]
    block_len = prompt_kv.shape[3]
    head_dim = prompt_kv.shape[4] // 2
    slots_sec = kept.shape[3]
    step_count = queries.shape[0]
    groups_local = queries.shape[3] // (heads_local * head_dim)
    picked = jnp.take_along_axis(prompt_kv, kept[:, :, 0, :, None, None], axis=2)
    entries = lax.broadcasted_iota(jnp.int32, (rows_group, heads_local, slots_sec), 2)
    live_mask = (entries < live_count[:, :, None]).astype(jnp.bfloat16)
    arrived, live_flags = (
        lax.all_to_all(
            lax.all_to_all(picked, "pre", split_axis=0, concat_axis=2, tiled=True),
            "cache",
            split_axis=2,
            concat_axis=0,
            tiled=True,
        ),
        lax.all_to_all(
            lax.all_to_all(live_mask, "pre", split_axis=0, concat_axis=2, tiled=True),
            "cache",
            split_axis=2,
            concat_axis=0,
            tiled=True,
        ),
    )
    row_count = arrived.shape[0]
    tokens = arrived.shape[2] * block_len
    key_rows = arrived[..., :head_dim].reshape(row_count, heads_local, tokens, head_dim)
    values = arrived[..., head_dim:].reshape(row_count, heads_local, tokens, head_dim)
    tok_mask = jnp.repeat(live_flags > 0, block_len, axis=2)
    query_rows = queries.reshape(step_count, row_count, heads_local, groups_local, head_dim)
    partials = partial_softmax(query_rows, key_rows, values, tok_mask)
    maxima, totals, weighted = combined_all(partials, "cache", combine_parts)
    attention = (weighted / totals[..., None]).astype(jnp.bfloat16)
    attention = attention.reshape(step_count * row_count, heads_local * groups_local * head_dim)
    weight = out_weight.reshape(out_weight.shape[0], -1)
    out_terms = jnp.dot(attention, weight, preferred_element_type=jnp.float32)
    summed = lax.psum_scatter(
        out_terms.astype(jnp.bfloat16), "head", scatter_dimension=1, tiled=True
    )
    attended = summed.reshape(step_count, queries.shape[1], queries.shape[2], -1)
    floats = prefill_x.astype(jnp.float32)
    inverse = lax.rsqrt(jnp.mean(floats * floats, axis=-1, keepdims=True) + 1e-05)
    normed = (floats * inverse * prefill_gain.astype(jnp.float32)).astype(jnp.bfloat16)
    next_kv = jnp.dot(
        normed, kv_weight.reshape(kv_weight.shape[0], -1), preferred_element_type=jnp.float32
    )
    next_kv = next_kv.astype(jnp.bfloat16).reshape(
        prefill_x.shape[0], kv_weight.shape[1], kv_weight.shape[2]
    )
    return (attended, next_kv)


def solution(mesh):
    in_specs = (
        P("cache", "head", "pre", None, None),
        P("cache", "head", "pre", None),
        P("cache", "head"),
        P(None, None, "pre", "head"),
        P("head", None, "cache", None),
        P(("pre", "cache"), None),
        P(),
        P(None, "head", None),
    )
    out_specs = (P(None, None, "pre", ("head", "cache")), P(("pre", "cache"), "head", None))
    return jax.shard_map(body, mesh=mesh, in_specs=in_specs, out_specs=out_specs, check_vma=False)
```

profile of v0, /device:TPU:1, one launch (start us, length us, event | category | flops | bytes accessed | tf_op | source)
XLA Modules:
  0.0 164.6 jit_solution(12413766092688453595)
XLA Ops:
  7.2 1.3 compare_convert_fusion
  8.5 4.8 %all-to-all-start = ((bf16[4,1,8]{2,1,0:T(2,128)(2,1)}), bf16[4,1,8]{2,1,0:T(2,128)(2,1)S(1)}, u32[]{:S(2)}, u32[]{:S(2)}) async-start(bf16[4,1,8]{2,1,0:T(2,128)(2,1)} %compare_convert_fusion), calls=%async_computation | async-start | bytes 4096 | tf_op jit(solution)/shard_map/all_to_all | solution.py:68
  13.3 0.7 fusion.35
  14.1 0.7 compare_and_fusion
  14.8 5.4 %gather_fusion = bf16[32,128,256]{2,1,0:T(8,128)(2,1)} fusion(bf16[4,32,128,256]{3,2,1,0:T(8,128)(2,1)} %bitcast.117, s32[32]{0:T(128)S(1)} %reshape.241), kind=kCustom, calls=%fused_computation | custom fusion | bytes 4194560 | tf_op jit(solution)/shard_map/jit(take_along_axis)/gather | solution.py:56
  20.2 1.8 %broadcast_select_fusion = bf16[4,1,8,128,256]{4,3,2,1,0:T(8,128)(2,1)S(1)} fusion(bf16[4,1,8,128,256]{4,3,2,1,0:T(8,128)(2,1)} %bitcast.112, pred[4,8]{1,0:T(4,128)(4,1)S(1)} %compare_and_fusion), kind=kLoop, calls=%fused_computation.23 | loop fusion | flops 1048576 | bytes 4194336 | tf_op jit(solution)/shard_map/jit(take_along_axis)/select_n | solution.py:56
  22.2 9.0 %all_to_all.46 = bf16[1,1,32]{1,0,2:T(2,128)(2,1)S(1)} all-to-all(bf16[1,1,32]{1,0,2:T(2,128)(2,1)S(1)} %all_to_all.41), channel_id=1, replica_groups=mesh['pre'=4,'head'=8,'cache'=4] {'cache'}, dimensions={2} | all-to-all | bytes 128 | tf_op jit(solution)/shard_map/all_to_all | solution.py:67
  31.2 27.6 %all_to_all.47 = bf16[4,1,8,128,256]{4,3,2,1,0:T(8,128)(2,1)} all-to-all(bf16[4,1,8,128,256]{4,3,2,1,0:T(8,128)(2,1)S(1)} %broadcast_select_fusion), channel_id=1, replica_groups=mesh['pre'=4,'head'=8,'cache'=4] {'pre'}, dimensions={0} | all-to-all | bytes 4194304 | tf_op jit(solution)/shard_map/all_to_all | solution.py:61
  58.8 3.6 %all-to-all-start.3 = ((bf16[1,1,32,128,256]{4,3,1,0,2:T(8,128)(2,1)}), bf16[1,1,32,128,256]{4,3,1,0,2:T(8,128)(2,1)S(1)}, u32[]{:S(2)}, u32[]{:S(2)}) async-start(bf16[1,1,32,128,256]{4,3,1,0,2:T(8,128)(2,1)} %bitcast.111), calls=%async_computation.3 | async-start | bytes 4194304 | tf_op jit(solution)/shard_map/all_to_all | solution.py:60
  62.5 5.6 %copy.40 = bf16[128,8,8,256]{3,1,2,0:T(8,128)(2,1)} copy(bf16[128,8,8,256]{3,2,1,0:T(8,128)(2,1)} %bitcast.113) | data formatting | bytes 8388608
  68.1 5.1 %fusion.6 = f32[512]{0:T(512)S(1)} fusion(bf16[512,8192]{1,0:T(8,128)(2,1)} %param.15), kind=kLoop, calls=%fused_computation.15 | loop fusion | flops 12582400 | bytes 8390656 | tf_op jit(solution)/shard_map/reduce_sum | solution.py:92
  73.2 0.7 compare_reduce_fusion
  74.1 10.7 %all-to-all-done.3 = bf16[1,1,32,128,256]{4,3,1,0,2:T(8,128)(2,1)S(1)} async-done(((bf16[1,1,32,128,256]{4,3,1,0,2:T(8,128)(2,1)}), bf16[1,1,32,128,256]{4,3,1,0,2:T(8,128)(2,1)S(1)}, u32[]{:S(2)}, u32[]{:S(2)}) %all-to-all-start.3) | async-done | bytes 2097184 | tf_op jit(solution)/shard_map/all_to_all | solution.py:60
  84.8 0.6 fusion.36
  85.4 0.5 fusion.37
  86.1 0.3 convolution_bitcast_fusion
  86.4 9.2 %all-gather.2 = f32[12,4,1,8,128]{4,3,0,1,2:T(8,128)S(1)} all-gather(f32[3,4,1,8,128]{4,3,0,1,2:T(8,128)S(1)} %convolution_bitcast_fusion), channel_id=4, replica_groups=mesh['pre'=4,'head'=8,'cache'=4] {'cache'}, dimensions={0}, use_global_device_ids=true | all-gather | bytes 245760 | tf_op jit(solution)/shard_map/all_gather | solution.py:10
  95.7 9.2 %all-gather.1 = f32[12,4,8]{2,1,0:T(4,128)S(1)} all-gather(f32[3,4,8]{2,1,0:T(4,128)S(1)} %copy.29), channel_id=3, replica_groups=mesh['pre'=4,'head'=8,'cache'=4] {'cache'}, dimensions={0}, use_global_device_ids=true | all-gather | bytes 1920 | tf_op jit(solution)/shard_map/all_gather | solution.py:10
  104.9 9.0 %all-gather = f32[12,4,8]{2,1,0:T(4,128)S(1)} all-gather(f32[3,4,8]{2,1,0:T(4,128)S(1)} %copy.28), channel_id=2, replica_groups=mesh['pre'=4,'head'=8,'cache'=4] {'cache'}, dimensions={0}, use_global_device_ids=true | all-gather | bytes 1920 | tf_op jit(solution)/shard_map/all_gather | solution.py:10
  114.0 0.5 while.19
  114.6 3.5 %convolution_convert_fusion = bf16[12,2048]{1,0:T(8,128)(2,1)} fusion(bf16[12,1024]{1,0:T(8,128)(2,1)S(1)} %bitcast.121, bf16[1024,2048]{1,0:T(8,128)(2,1)} %bitcast.109), kind=kOutput, calls=%fused_computation.22 | convolution fusion | flops 50356224 | bytes 4268032 | tf_op jit(solution)/shard_map/dot_general | solution.py:86
  118.1 7.7 %fusion.20 = bf16[512,1,256]{2,0,1:T(8,128)(2,1)} fusion(bf16[8192,1,256]{2,0,1:T(8,128)(2,1)} %param.17, bf16[512,8192]{1,0:T(8,128)(2,1)} %param.15, f32[8192]{0:T(1024)S(1)} %convert_element_type.37, f32[512]{0:T(512)S(1)} %add_rsqrt_fusion), kind=kOutput, calls=%fused_computation.27 | convolution fusion | flops 2164391936 | bytes 12879872 | tf_op jit(solution)/shard_map/dot_general | solution.py:94
  125.8 30.6 %reduce-scatter.2.cloned.1.call-done = bf16[12,256]{1,0:T(8,128)(2,1)} async-done(((bf16[12,2048]{1,0:T(8,128)(2,1)}), bf16[12,256]{1,0:T(8,128)(2,1)}) %reduce-scatter.2.cloned.1.call-update) | async-done | bytes 6160 | tf_op jit(solution)/shard_map/reduce_scatter | solution.py:87
  156.4 1.3 reshape.236
  (38 shorter events, 1.2 us)
Async XLA Ops:
  8.5 13.6 %all-to-all-start = ((bf16[4,1,8]{2,1,0:T(2,128)(2,1)}), bf16[4,1,8]{2,1,0:T(2,128)(2,1)S(1)}, u32[]{:S(2)}, u32[]{:S(2)}) async-start(bf16[4,1,8]{2,1,0:T(2,128)(2,1)} %compare_convert_fusion), calls=%async_computation | async-start | bytes 4096 | tf_op jit(solution)/shard_map/all_to_all | solution.py:68
  31.2 31.3 %copy-start = (bf16[3,4,1,1024]{3,1,2,0:T(4,128)(2,1)S(1)}, bf16[3,4,1,1024]{3,1,2,0:T(4,128)(2,1)}, u32[]{:S(2)}) copy-start(bf16[3,4,1,1024]{3,1,2,0:T(4,128)(2,1)} %param.13) | copy-start | bytes 73732
  58.8 26.0 %all-to-all-start.3 = ((bf16[1,1,32,128,256]{4,3,1,0,2:T(8,128)(2,1)}), bf16[1,1,32,128,256]{4,3,1,0,2:T(8,128)(2,1)S(1)}, u32[]{:S(2)}, u32[]{:S(2)}) async-start(bf16[1,1,32,128,256]{4,3,1,0,2:T(8,128)(2,1)} %bitcast.111), calls=%async_computation.3 | async-start | bytes 4194304 | tf_op jit(solution)/shard_map/all_to_all | solution.py:60
  62.4 94.0 %reduce-scatter.2.cloned.1.call-start = ((), (), s32[]{:S(2)}) async-start(), calls=%async_computation.5 | async-start | bytes 73728 | tf_op jit(solution)/shard_map/reduce_scatter | solution.py:87
  62.5 5.6 %copy-start.1 = (bf16[8192]{0:T(1024)(128)(2,1)S(1)}, bf16[8192]{0:T(1024)(128)(2,1)}, u32[]{:S(2)}) copy-start(bf16[8192]{0:T(1024)(128)(2,1)} %param.16) | copy-start | bytes 49156
Sparse Core Ops, SparseCore 0:
  118.3 38.1 reduce-scatter.1
where the time goes:
time: 167 us; the launch traced here: 165 us
  blocking collectives  64.1 us (38%)
  waiting for transfers between devices  41.3 us (25%)
  between operations  14.1 us (8%)
  local copies, waits for them, and re-layouts  13.3 us (8%)
  matrix products  12 us (7%)
  other arithmetic  11.1 us (7%)
  starting transfers between devices  8.49 us (5%)
    reduce_scatter x1, waiting for transfers between devices, body(): lax.psum_scatter(out_terms.astype(jnp.bfloat16), 'head', scatter_dimensio...  30.6 us
    all_to_all x1, blocking collectives, body(): lax.all_to_all(picked, 'pre', split_axis=0, concat_axis=2, tiled=True)  27.6 us
    all_gather x3, blocking collectives, combined_all(): gathered = jax.tree.map(lambda a: lax.all_gather(a, axis), part)  27.5 us
    all_to_all x1, waiting for transfers between devices, body(): lax.all_to_all(lax.all_to_all(picked, 'pre', split_axis=0, concat_axis=2,...  10.7 us
    all_to_all x1, blocking collectives, body(): lax.all_to_all(lax.all_to_all(live_mask, 'pre', split_axis=0, concat_axis...  9.03 us
    dot_general x1, matrix products, body(): jnp.dot(normed, kv_weight.reshape(kv_weight.shape[0], -1), preferred_elem...  7.68 us
    unnamed x9, local copies, waits for them, and re-layouts  5.71 us
    gather x2, local copies, waits for them, and re-layouts, body(): jnp.take_along_axis(prompt_kv, kept[:, :, 0, :, None, None], axis=2)  5.5 us
  transfers between devices with their start and end apart: 3, of which 2 were waited for; matrix products, arithmetic and copies ran while one was open for 17% of the time, Pallas kernels for 0%

commit v1 on v0

v1 whole, which is shorter than its diff:
```python
import functools
import math

import jax
import jax.numpy as jnp
from jax import lax
from jax.experimental import pallas as pl
from jax.experimental.pallas import tpu as pltpu
from jax.sharding import PartitionSpec as P

F32 = jnp.float32
BF16 = jnp.bfloat16
VMEM = pl.BlockSpec(memory_space=pltpu.VMEM)
SMEM = pl.BlockSpec(memory_space=pltpu.SMEM)
ANY = pl.BlockSpec(memory_space=pl.ANY)

PRE, HEAD, CACHE = 4, 8, 4
STEPS = 3
SLOT = 4
GROUP = 8
HD = 128
BLK = 128
KS = 8
EPS = 1e-05


def prefill_kernel(x_ref, gain_ref, w_ref, out_ref, acc, squares):
    step = pl.program_id(0)

    @pl.when(step == 0)
    def _():
        acc[...] = jnp.zeros_like(acc)
        squares[...] = jnp.zeros_like(squares)

    x = x_ref[...]
    floats = x.astype(F32)
    sq = floats * floats
    part = squares[...]
    for k in range(x.shape[1] // 128):
        part = part + sq[:, k * 128 : (k + 1) * 128]
    squares[...] = part
    acc[...] += jnp.dot(x * gain_ref[...], w_ref[...], preferred_element_type=F32)

    @pl.when(step == pl.num_programs(0) - 1)
    def _():
        mean = jnp.sum(squares[...], axis=1, keepdims=True) * (1.0 / 8192.0)
        out_ref[...] = (acc[...] * lax.rsqrt(mean + EPS)).astype(BF16)


def prefill(x, gain, w):
    rows, width = x.shape
    cols = w.shape[1]
    depth = 1024
    return pl.pallas_call(
        prefill_kernel,
        grid=(width // depth,),
        in_specs=[
            pl.BlockSpec((rows, depth), lambda k: (0, k)),
            pl.BlockSpec((1, depth), lambda k: (0, k)),
            pl.BlockSpec((depth, cols), lambda k: (k, 0)),
        ],
        out_specs=pl.BlockSpec((rows, cols), lambda k: (0, 0)),
        out_shape=jax.ShapeDtypeStruct((rows, cols), BF16),
        scratch_shapes=[pltpu.VMEM((rows, cols), F32), pltpu.VMEM((rows, 128), F32)],
        compiler_params=pltpu.CompilerParams(vmem_limit_bytes=32 * 1024 * 1024),
        cost_estimate=pl.CostEstimate(
            flops=2 * rows * width * cols,
            bytes_accessed=2 * (rows * width + width * cols + rows * cols),
            transcendentals=0,
        ),
        name="prefill",
    )(x, gain, w)


def attend_kernel(kept, live, q0, q1, q2, q3, kv_hbm, out_ref, kv, qs, sems):
    mine = lax.axis_index("pre")
    group = lax.axis_index("cache")
    copies = []
    for k in range(PRE):
        request = mine ^ k
        row = []
        for t in range(KS):
            copy = pltpu.make_async_copy(
                kv_hbm.at[request, 0, kept[request, t]], kv.at[k, t], sems.at[k, t]
            )
            copy.start()
            row.append(copy)
        copies.append(row)
    rows = GROUP * SLOT
    lane = lax.broadcasted_iota(jnp.int32, (rows, HD), 1)
    step_of = lax.broadcasted_iota(jnp.int32, (rows, HD), 0) % SLOT
    token = lax.broadcasted_iota(jnp.int32, (rows, KS * BLK), 1)
    at_group = lax.broadcasted_iota(jnp.int32, (STEPS, CACHE, GROUP * HD), 1) == group
    for k, q_ref in enumerate((q0, q1, q2, q3)):
        request = mine ^ k
        q = jnp.sum(jnp.where(at_group, q_ref[...].astype(F32), 0.0), axis=1)
        q = jnp.concatenate([q, jnp.zeros((SLOT - STEPS, GROUP * HD), F32)], axis=0)
        for j in range(GROUP):
            qs[k, j * SLOT : (j + 1) * SLOT, :] = q[:, j * HD : (j + 1) * HD]
        for copy in copies[k]:
            copy.wait()
        keys = kv[k, :, :, :HD].reshape(KS * BLK, HD)
        values = kv[k, :, :, HD:].reshape(KS * BLK, HD)
        scores = lax.dot_general(
            qs[k].astype(BF16), keys, (((1,), (1,)), ((), ())), preferred_element_type=F32
        ) * (1.0 / math.sqrt(HD))
        alive = token < live[request] * BLK
        scores = jnp.where(alive, scores, -1e30)
        top = jnp.max(scores, axis=1, keepdims=True).astype(BF16).astype(F32)
        terms = jnp.exp(scores - top)
        total = jnp.sum(terms, axis=1, keepdims=True)
        weighted = jnp.dot(terms.astype(BF16), values, preferred_element_type=F32) / total
        high = total.astype(BF16).astype(F32)
        figures = jnp.where(lane == step_of, top, 0.0)
        figures = jnp.where(lane == step_of + SLOT, high, figures)
        figures = jnp.where(lane == step_of + 2 * SLOT, total - high, figures)
        figures = (
            pltpu.roll(figures, 1, 0) + pltpu.roll(figures, 2, 0) + pltpu.roll(figures, 3, 0)
        )
        message = jnp.where(step_of == STEPS, figures, weighted).astype(BF16)
        for c in range(CACHE):
            out_ref[request * CACHE + c] = message


def attend(kept, live, queries, kv):
    return pl.pallas_call(
        attend_kernel,
        in_specs=[SMEM, SMEM, VMEM, VMEM, VMEM, VMEM, ANY],
        out_specs=VMEM,
        out_shape=jax.ShapeDtypeStruct((PRE * CACHE, GROUP * SLOT, HD), BF16),
        scratch_shapes=[
            pltpu.VMEM((PRE, KS, BLK, 2 * HD), BF16),
            pltpu.VMEM((PRE, GROUP * SLOT, HD), F32),
            pltpu.SemaphoreType.DMA((PRE, KS)),
        ],
        compiler_params=pltpu.CompilerParams(vmem_limit_bytes=16 * 1024 * 1024),
        cost_estimate=pl.CostEstimate(
            flops=2 * PRE * 2 * 32 * 1024 * 128, bytes_accessed=1 << 21, transcendentals=1 << 17
        ),
        name="attend",
    )(kept, live, *queries, kv)


def project_kernel(parts_ref, w_ref, out_ref, sheet):
    rows = GROUP * SLOT
    lane = lax.broadcasted_iota(jnp.int32, (rows, HD), 1)
    step_of = lax.broadcasted_iota(jnp.int32, (rows, HD), 0) % SLOT
    for c in range(CACHE):
        tops, totals, values = [], [], []
        for p in range(PRE):
            part = parts_ref[p * CACHE + c].astype(F32)
            figures = jnp.where(step_of == STEPS, part, 0.0)
            figures = (
                pltpu.roll(figures, rows - 1, 0)
                + pltpu.roll(figures, rows - 2, 0)
                + pltpu.roll(figures, rows - 3, 0)
            )
            tops.append(
                jnp.sum(jnp.where(lane == step_of, figures, 0.0), axis=1, keepdims=True)
            )
            totals.append(
                jnp.sum(
                    jnp.where(
                        (lane == step_of + SLOT) | (lane == step_of + 2 * SLOT), figures, 0.0
                    ),
                    axis=1,
                    keepdims=True,
                )
            )
            values.append(part)
        top = functools.reduce(jnp.maximum, tops)
        shares = [jnp.exp(t - top) * total for t, total in zip(tops, totals)]
        scale = 1.0 / functools.reduce(jnp.add, shares)
        joined = functools.reduce(
            jnp.add, [(share * scale) * value for share, value in zip(shares, values)]
        )
        joined = jnp.where(step_of == STEPS, 0.0, joined)
        for j in range(GROUP):
            sheet[j, c * SLOT : (c + 1) * SLOT, :] = joined[j * SLOT : (j + 1) * SLOT, :]
    wide = HD * HEAD
    spread = (
        lax.broadcasted_iota(jnp.int32, (HD, wide), 1) // HEAD
        == lax.broadcasted_iota(jnp.int32, (HD, wide), 0)
    ).astype(BF16)
    repeated = jnp.dot(
        sheet[...].reshape(GROUP * CACHE * SLOT, HD).astype(BF16),
        spread,
        preferred_element_type=F32,
    ).astype(BF16)
    block = lax.broadcasted_iota(jnp.int32, (CACHE * SLOT, wide), 1) % HEAD
    total = jnp.zeros((HEAD * CACHE * SLOT, out_ref.shape[2]), F32)
    for j in range(GROUP):
        rows_j = repeated[j * CACHE * SLOT : (j + 1) * CACHE * SLOT, :]
        lhs = jnp.concatenate(
            [jnp.where(block == h, rows_j, jnp.zeros_like(rows_j)) for h in range(HEAD)], axis=0
        )
        total = total + jnp.dot(
            lhs, w_ref[j * wide : (j + 1) * wide, :], preferred_element_type=F32
        )
    out_ref[...] = total.reshape(out_ref.shape).astype(BF16)


def project(parts, weight):
    cols = weight.shape[1]
    return pl.pallas_call(
        project_kernel,
        in_specs=[VMEM, VMEM],
        out_specs=VMEM,
        out_shape=jax.ShapeDtypeStruct((HEAD, CACHE * SLOT, cols), BF16),
        scratch_shapes=[pltpu.VMEM((GROUP, CACHE * SLOT, HD), F32)],
        compiler_params=pltpu.CompilerParams(vmem_limit_bytes=24 * 1024 * 1024),
        cost_estimate=pl.CostEstimate(
            flops=2 * 128 * 8192 * 256, bytes_accessed=1 << 22, transcendentals=0
        ),
        name="project",
    )(parts, weight)


def total_kernel(terms_ref, out_ref, sheet):
    for n in range(terms_ref.shape[2] // 128):
        lanes = slice(n * 128, (n + 1) * 128)
        sheet[n] = jnp.sum(terms_ref[:, :, lanes].astype(F32), axis=0)
        for s in range(STEPS):
            out_ref[s, :, lanes] = sheet[n, pl.ds(s, CACHE, stride=SLOT), :].astype(BF16)


def total_of(terms):
    cols = terms.shape[2]
    return pl.pallas_call(
        total_kernel,
        in_specs=[VMEM],
        out_specs=VMEM,
        out_shape=jax.ShapeDtypeStruct((STEPS, CACHE, cols), BF16),
        scratch_shapes=[pltpu.VMEM((cols // 128, CACHE * SLOT, 128), F32)],
        name="total",
    )(terms)


def body(prompt_kv, kept, live_count, queries, out_weight, prefill_x, prefill_gain, kv_weight):
    queries = queries.reshape(STEPS, CACHE, GROUP * HD)
    around = [queries]
    for k in (2, 1, 3):
        around.append(lax.ppermute(queries, "pre", [(i, i ^ k) for i in range(PRE)]))
    around = [around[0], around[2], around[1], around[3]]
    parts = attend(kept.reshape(PRE, KS), live_count.reshape(PRE), around, prompt_kv)
    parts = lax.all_to_all(parts, ("pre", "cache"), split_axis=0, concat_axis=0, tiled=True)
    next_kv = prefill(prefill_x, prefill_gain.reshape(1, -1), kv_weight.reshape(8192, 256))
    terms = project(parts, out_weight.reshape(8192, 256))
    terms = lax.all_to_all(terms, "head", split_axis=0, concat_axis=0, tiled=True)
    attended = total_of(terms)
    return (attended.reshape(STEPS, CACHE, 1, 256), next_kv.reshape(512, 1, 256))


def solution(mesh):
    in_specs = (
        P("cache", "head", "pre", None, None),
        P("cache", "head", "pre", None),
        P("cache", "head"),
        P(None, None, "pre", "head"),
        P("head", None, "cache", None),
        P(("pre", "cache"), None),
        P(),
        P(None, "head", None),
    )
    out_specs = (P(None, None, "pre", ("head", "cache")), P(("pre", "cache"), "head", None))
    return jax.shard_map(body, mesh=mesh, in_specs=in_specs, out_specs=out_specs, check_vma=False)
```

time: 167 us -> 58.5 us (0.35); the launches traced: 165 us -> 58 us
  blocking collectives: 64.1 us -> 0 us
  waiting for transfers between devices: 41.3 us -> 10.7 us
  Pallas kernels: 0 us -> 14.7 us
  between operations: 14.1 us -> 0.68 us
  matrix products: 12 us -> 0 us
  other arithmetic: 11.1 us -> 0 us
  starting transfers between devices: 8.49 us -> 18 us
    all_to_all x2 -> x0, blocking collectives: 36.6 us -> none  [the longest x1 27.6 us: body(): lax.all_to_all(picked, 'pre', split_axis=0, concat_axis=2, tiled=True)]
    reduce_scatter x1 -> x0, waiting for transfers between devices: 30.6 us -> none  [body(): lax.psum_scatter(out_terms.astype(jnp.bfloat16), 'head', scatter_dimensio...]
    all_gather x3 -> x0, blocking collectives: 27.5 us -> none  [combined_all(): gathered = jax.tree.map(lambda a: lax.all_gather(a, axis), part)]
    pallas_call x0 -> x4, Pallas kernels: none -> 14.7 us  [the longest x1 6.24 us: attend(): pl.pallas_call(attend_kernel, in_specs=[SMEM, SMEM, VMEM, VMEM, VMEM, VME...]
    dot_general x4 -> x0, matrix products: 12 us -> none  [the longest x1 7.68 us: body(): jnp.dot(normed, kv_weight.reshape(kv_weight.shape[0], -1), preferred_elem...]
    unnamed x9 -> x18, local copies, waits for them, and re-layouts: 5.71 us -> 13.8 us
    gather x2 -> x0, local copies, waits for them, and re-layouts: 5.5 us -> none  [body(): jnp.take_along_axis(prompt_kv, kept[:, :, 0, :, None, None], axis=2)]
    reduce_sum x2 -> x0, other arithmetic: 5.32 us -> none  [the longest x1 5.1 us: body(): jnp.mean(floats * floats, axis=-1, keepdims=True) + 1e-05]
  transfers between devices with their start and end apart: 3 -> 5, of which waited for: 2 -> 3; matrix products, arithmetic and copies ran while one was open for 17% -> 0% of each run, Pallas kernels for 0% -> 9%
where the time goes in v1:
time: 58.5 us; the launch traced here: 58 us
  starting transfers between devices  18 us (31%)
  Pallas kernels  14.7 us (25%)
  local copies, waits for them, and re-layouts  13.9 us (24%)
  waiting for transfers between devices  10.7 us (18%)
  between operations  0.68 us (1%)
    unnamed x18, local copies, waits for them, and re-layouts  13.8 us
    all_to_all x1, starting transfers between devices, body(): lax.all_to_all(terms, 'head', split_axis=0, concat_axis=0, tiled=True)  8.27 us
    all_to_all x1, waiting for transfers between devices, body(): lax.all_to_all(parts, ('pre', 'cache'), split_axis=0, concat_axis=0, tile...  6.65 us
    pallas_call x1, Pallas kernels, attend(): pl.pallas_call(attend_kernel, in_specs=[SMEM, SMEM, VMEM, VMEM, VMEM, VME...  6.24 us
    pallas_call x1, Pallas kernels, prefill(): pl.pallas_call(prefill_kernel, grid=(width // depth,), in_specs=[pl.Block...  5.2 us
    all_to_all x1, starting transfers between devices, body(): lax.all_to_all(parts, ('pre', 'cache'), split_axis=0, concat_axis=0, tile...  5.16 us
    ppermute x3, starting transfers between devices, body(): lax.ppermute(queries, 'pre', [(i, i ^ k) for i in range(PRE)])  4.6 us
    ppermute x3, waiting for transfers between devices, body(): lax.ppermute(queries, 'pre', [(i, i ^ k) for i in range(PRE)])  4.06 us
  transfers between devices with their start and end apart: 5, of which 3 were waited for; matrix products, arithmetic and copies ran while one was open for 0% of the time, Pallas kernels for 9%

profile of v1, /device:TPU:1, one launch (start us, length us, event | category | flops | bytes accessed | tf_op | source)
XLA Modules:
  0.0 58.0 jit_solution(17399691300162870059)
XLA Ops:
  0.6 2.1 %collective-permute-start = (bf16[3,4,1024]{2,1,0:T(4,128)(2,1)}, bf16[3,4,1024]{2,1,0:T(4,128)(2,1)S(1)}, u32[]{:S(2)}, u32[]{:S(2)}) collective-permute-start(bf16[3,4,1024]{2,1,0:T(4,128)(2,1)} %bitcast.11), channel_id=1, source_target_pairs={{0,32},{32,0},{64,96},{96,64},{1,33},{33,1},{65,97},{97,65},{2,34}... | collective-permute-start | bytes 73736 | tf_op jit(solution)/shard_map/ppermute | solution.py:243
  2.8 2.5 %collective-permute-start.1 = (bf16[3,4,1024]{2,1,0:T(4,128)(2,1)}, bf16[3,4,1024]{2,1,0:T(4,128)(2,1)S(1)}, u32[]{:S(2)}, u32[]{:S(2)}) collective-permute-start(bf16[3,4,1024]{2,1,0:T(4,128)(2,1)} %bitcast.12), channel_id=1, source_target_pairs={{0,64},{32,96},{64,0},{96,32},{1,65},{33,97},{65,1},{97,33},{2,66}... | collective-permute-start | bytes 73736 | tf_op jit(solution)/shard_map/ppermute | solution.py:243
  5.2 0.0 collective-permute-start.2
  5.2 0.0 collective-permute-done.q1
  5.2 1.9 %collective-permute-done.1.q2 = bf16[3,4,1024]{2,1,0:T(4,128)(2,1)S(1)} collective-permute-done((bf16[3,4,1024]{2,1,0:T(4,128)(2,1)}, bf16[3,4,1024]{2,1,0:T(4,128)(2,1)S(1)}, u32[]{:S(2)}, u32[]{:S(2)}) %collective-permute-start.1) | collective-permute-done | bytes 24608 | tf_op jit(solution)/shard_map/ppermute | solution.py:243
  7.1 2.2 %collective-permute-done.2.q3 = bf16[3,4,1024]{2,1,0:T(4,128)(2,1)S(1)} collective-permute-done((bf16[3,4,1024]{2,1,0:T(4,128)(2,1)}, bf16[3,4,1024]{2,1,0:T(4,128)(2,1)S(1)}, u32[]{:S(2)}, u32[]{:S(2)}) %collective-permute-start.2) | collective-permute-done | bytes 24608 | tf_op jit(solution)/shard_map/ppermute | solution.py:243
  9.3 0.0 copy-start
  9.3 3.4 %copy-done = bf16[4,1,32,128,256]{4,3,2,1,0:T(8,128)(2,1)S(1)} copy-done((bf16[4,1,32,128,256]{4,3,2,1,0:T(8,128)(2,1)S(1)}, bf16[4,1,32,128,256]{4,3,2,1,0:T(8,128)(2,1)}, u32[]{:S(2)}) %copy-start) | copy-done | bytes 8388632
  12.7 0.7 %copy-done.4 = bf16[3,4,1,1024]{3,1,2,0:T(4,128)(2,1)S(1)} copy-done((bf16[3,4,1,1024]{3,1,2,0:T(4,128)(2,1)S(1)}, bf16[3,4,1,1024]{3,1,2,0:T(4,128)(2,1)}, u32[]{:S(2)}) %copy-start.4) | copy-done | bytes 24600
  13.4 0.7 %copy-done.5 = s32[4,1,1,8]{3,2,1,0:T(1,128)S(1)} copy-done((s32[4,1,1,8]{3,2,1,0:T(1,128)S(1)}, s32[4,1,1,8]{3,2,1,0:T(1,128)}, u32[]{:S(2)}) %copy-start.5) | copy-done | bytes 152
  14.1 0.7 %copy-done.6 = s32[4,1]{0,1:T(1,128)S(1)} copy-done((s32[4,1]{0,1:T(1,128)S(1)}, s32[4,1]{0,1:T(1,128)}, u32[]{:S(2)}) %copy-start.6) | copy-done | bytes 40
  14.8 6.2 %attend.1 = bf16[16,32,128]{2,1,0:T(8,128)(2,1)} custom-call(s32[4,8]{1,0:T(4,128)S(1)} %bitcast.15, s32[4]{0:T(128)S(1)} %bitcast.16, bf16[3,4,1024]{2,1,0:T(4,128)(2,1)S(1)} %bitcast.14, bf16[3,4,1024]{2,1,0:T(4,128)(2,1)S(1)} %collective-permute-done.q1, bf16[3,4,1024]{2,1,0:T(4,128)(2,1)S(1)} %collective-permute-done.1.q2, ...), custom_call_target="tpu_custom_call" | custom-call | flops 67108864 | bytes 2097152 | tf_op jit(solution)/shard_map/attend/pallas_call | solution.py:126
  21.0 5.2 %all-to-all-start = ((bf16[16,32,128]{2,1,0:T(8,128)(2,1)}), bf16[16,32,128]{2,1,0:T(8,128)(2,1)S(1)}, u32[]{:S(2)}, u32[]{:S(2)}) async-start(bf16[16,32,128]{2,1,0:T(8,128)(2,1)} %attend.1), calls=%async_computation | async-start | bytes 262144 | tf_op jit(solution)/shard_map/all_to_all | solution.py:246
  26.2 0.0 copy-done.8
  26.2 6.7 %all-to-all-done.parts_ref = bf16[16,32,128]{2,1,0:T(8,128)(2,1)S(1)} async-done(((bf16[16,32,128]{2,1,0:T(8,128)(2,1)}), bf16[16,32,128]{2,1,0:T(8,128)(2,1)S(1)}, u32[]{:S(2)}, u32[]{:S(2)}) %all-to-all-start) | async-done | bytes 131104 | tf_op jit(solution)/shard_map/all_to_all | solution.py:246
  32.9 2.2 %copy-done.3 = bf16[1024,8,1,256]{3,1,2,0:T(8,128)(2,1)S(1)} copy-done((bf16[1024,8,1,256]{3,1,2,0:T(8,128)(2,1)S(1)}, bf16[1024,8,1,256]{3,1,2,0:T(8,128)(2,1)}, u32[]{:S(2)}) %copy-start.3) | copy-done | bytes 4194328
  35.1 1.8 %project.1 = bf16[8,16,256]{2,1,0:T(8,128)(2,1)} custom-call(bf16[16,32,128]{2,1,0:T(8,128)(2,1)S(1)} %all-to-all-done.parts_ref, bf16[8192,256]{1,0:T(8,128)(2,1)S(1)} %bitcast.10), custom_call_target="tpu_custom_call" | custom-call | flops 536870912 | bytes 4194304 | tf_op jit(solution)/shard_map/project/pallas_call | solution.py:205
  36.8 8.3 %all-to-all-start.1 = ((bf16[8,16,256]{2,1,0:T(8,128)(2,1)}), bf16[8,16,256]{2,1,0:T(8,128)(2,1)S(1)}, u32[]{:S(2)}, u32[]{:S(2)}) async-start(bf16[8,16,256]{2,1,0:T(8,128)(2,1)} %project.1), calls=%async_computation.1 | async-start | bytes 131072 | tf_op jit(solution)/shard_map/all_to_all | solution.py:249
  45.1 3.4 %copy-done.1 = bf16[512,8192]{1,0:T(8,128)(2,1)S(1)} copy-done((bf16[512,8192]{1,0:T(8,128)(2,1)S(1)}, bf16[512,8192]{1,0:T(8,128)(2,1)}, u32[]{:S(2)}) %copy-start.1) | copy-done | bytes 8388632
  48.5 2.2 %copy-done.2 = bf16[8192,1,256]{2,0,1:T(8,128)(2,1)S(1)} copy-done((bf16[8192,1,256]{2,0,1:T(8,128)(2,1)S(1)}, bf16[8192,1,256]{2,0,1:T(8,128)(2,1)}, u32[]{:S(2)}) %copy-start.2) | copy-done | bytes 4194328
  50.7 5.2 %prefill.1 = bf16[512,256]{1,0:T(8,128)(2,1)} custom-call(bf16[512,8192]{1,0:T(8,128)(2,1)S(1)} %copy-done.1, bf16[1,8192]{1,0:T(2,128)(2,1)S(1)} %reshape.33.gain_ref, bf16[8192,256]{1,0:T(8,128)(2,1)S(1)} %bitcast.9), custom_call_target="tpu_custom_call" | custom-call | flops 2147483648 | bytes 12845056 | tf_op jit(solution)/shard_map/prefill/pallas_call | solution.py:54
  55.9 0.0 all-to-all-done.1.terms_ref
  55.9 0.6 %copy-done.7 = bf16[8,16,256]{2,1,0:T(8,128)(2,1)} copy-done((bf16[8,16,256]{2,1,0:T(8,128)(2,1)}, bf16[8,16,256]{2,1,0:T(8,128)(2,1)S(1)}, u32[]{:S(2)}) %copy-start.7) | copy-done | bytes 65560
  56.5 1.5 %total.1 = bf16[3,4,256]{2,1,0:T(4,128)(2,1)} custom-call(bf16[8,16,256]{2,1,0:T(8,128)(2,1)} %copy-done.7), custom_call_target="tpu_custom_call" | custom-call | tf_op jit(solution)/shard_map/total/pallas_call | solution.py:229
  (9 shorter events, 0.0 us)
Async XLA Ops:
  0.6 4.6 %collective-permute-start = (bf16[3,4,1024]{2,1,0:T(4,128)(2,1)}, bf16[3,4,1024]{2,1,0:T(4,128)(2,1)S(1)}, u32[]{:S(2)}, u32[]{:S(2)}) collective-permute-start(bf16[3,4,1024]{2,1,0:T(4,128)(2,1)} %bitcast.11), channel_id=1, source_target_pairs={{0,32},{32,0},{64,96},{96,64},{1,33},{33,1},{65,97},{97,65},{2,34}... | collective-permute-start | bytes 73736 | tf_op jit(solution)/shard_map/ppermute | solution.py:243
  2.8 4.4 %collective-permute-start.1 = (bf16[3,4,1024]{2,1,0:T(4,128)(2,1)}, bf16[3,4,1024]{2,1,0:T(4,128)(2,1)S(1)}, u32[]{:S(2)}, u32[]{:S(2)}) collective-permute-start(bf16[3,4,1024]{2,1,0:T(4,128)(2,1)} %bitcast.12), channel_id=1, source_target_pairs={{0,64},{32,96},{64,0},{96,32},{1,65},{33,97},{65,1},{97,33},{2,66}... | collective-permute-start | bytes 73736 | tf_op jit(solution)/shard_map/ppermute | solution.py:243
  5.2 4.1 %collective-permute-start.2 = (bf16[3,4,1024]{2,1,0:T(4,128)(2,1)}, bf16[3,4,1024]{2,1,0:T(4,128)(2,1)S(1)}, u32[]{:S(2)}, u32[]{:S(2)}) collective-permute-start(bf16[3,4,1024]{2,1,0:T(4,128)(2,1)} %bitcast.13), channel_id=1, source_target_pairs={{0,96},{32,64},{64,32},{96,0},{1,97},{33,65},{65,33},{97,1},{2,98}... | collective-permute-start | bytes 73736 | tf_op jit(solution)/shard_map/ppermute | solution.py:243
  9.3 3.4 %copy-start = (bf16[4,1,32,128,256]{4,3,2,1,0:T(8,128)(2,1)S(1)}, bf16[4,1,32,128,256]{4,3,2,1,0:T(8,128)(2,1)}, u32[]{:S(2)}) copy-start(bf16[4,1,32,128,256]{4,3,2,1,0:T(8,128)(2,1)} %kv_hbm.1) | copy-start | bytes 25165828
  12.7 0.7 %copy-start.4 = (bf16[3,4,1,1024]{3,1,2,0:T(4,128)(2,1)S(1)}, bf16[3,4,1,1024]{3,1,2,0:T(4,128)(2,1)}, u32[]{:S(2)}) copy-start(bf16[3,4,1,1024]{3,1,2,0:T(4,128)(2,1)} %param.11) | copy-start | bytes 73732
  13.4 0.7 %copy-start.5 = (s32[4,1,1,8]{3,2,1,0:T(1,128)S(1)}, s32[4,1,1,8]{3,2,1,0:T(1,128)}, u32[]{:S(2)}) copy-start(s32[4,1,1,8]{3,2,1,0:T(1,128)} %param.9) | copy-start | bytes 388
  14.1 0.7 %copy-start.6 = (s32[4,1]{0,1:T(1,128)S(1)}, s32[4,1]{0,1:T(1,128)}, u32[]{:S(2)}) copy-start(s32[4,1]{0,1:T(1,128)} %param.10) | copy-start | bytes 52
  14.8 11.4 %copy-start.8 = (bf16[8192]{0:T(1024)(128)(2,1)S(1)}, bf16[8192]{0:T(1024)(128)(2,1)}, u32[]{:S(2)}) copy-start(bf16[8192]{0:T(1024)(128)(2,1)} %param.14) | copy-start | bytes 49156
  21.0 11.9 %all-to-all-start = ((bf16[16,32,128]{2,1,0:T(8,128)(2,1)}), bf16[16,32,128]{2,1,0:T(8,128)(2,1)S(1)}, u32[]{:S(2)}, u32[]{:S(2)}) async-start(bf16[16,32,128]{2,1,0:T(8,128)(2,1)} %attend.1), calls=%async_computation | async-start | bytes 262144 | tf_op jit(solution)/shard_map/all_to_all | solution.py:246
  32.9 2.2 %copy-start.3 = (bf16[1024,8,1,256]{3,1,2,0:T(8,128)(2,1)S(1)}, bf16[1024,8,1,256]{3,1,2,0:T(8,128)(2,1)}, u32[]{:S(2)}) copy-start(bf16[1024,8,1,256]{3,1,2,0:T(8,128)(2,1)} %param.12) | copy-start | bytes 12582916
  36.8 19.0 %all-to-all-start.1 = ((bf16[8,16,256]{2,1,0:T(8,128)(2,1)}), bf16[8,16,256]{2,1,0:T(8,128)(2,1)S(1)}, u32[]{:S(2)}, u32[]{:S(2)}) async-start(bf16[8,16,256]{2,1,0:T(8,128)(2,1)} %project.1), calls=%async_computation.1 | async-start | bytes 131072 | tf_op jit(solution)/shard_map/all_to_all | solution.py:249
  45.1 3.4 %copy-start.1 = (bf16[512,8192]{1,0:T(8,128)(2,1)S(1)}, bf16[512,8192]{1,0:T(8,128)(2,1)}, u32[]{:S(2)}) copy-start(bf16[512,8192]{1,0:T(8,128)(2,1)} %x_ref.1) | copy-start | bytes 25165828
  48.5 2.2 %copy-start.2 = (bf16[8192,1,256]{2,0,1:T(8,128)(2,1)S(1)}, bf16[8192,1,256]{2,0,1:T(8,128)(2,1)}, u32[]{:S(2)}) copy-start(bf16[8192,1,256]{2,0,1:T(8,128)(2,1)} %param.15) | copy-start | bytes 12582916
  55.9 0.6 %copy-start.7 = (bf16[8,16,256]{2,1,0:T(8,128)(2,1)}, bf16[8,16,256]{2,1,0:T(8,128)(2,1)S(1)}, u32[]{:S(2)}) copy-start(bf16[8,16,256]{2,1,0:T(8,128)(2,1)S(1)} %all-to-all-done.1.terms_ref) | copy-start | bytes 196612

commit v2 on v1

v2 whole, which is shorter than its diff:
```python
import functools
import math

import jax
import jax.numpy as jnp
from jax import lax
from jax.experimental import pallas as pl
from jax.experimental.pallas import tpu as pltpu
from jax.sharding import PartitionSpec as P

F32 = jnp.float32
BF16 = jnp.bfloat16
VMEM = pl.BlockSpec(memory_space=pltpu.VMEM)
SMEM = pl.BlockSpec(memory_space=pltpu.SMEM)
HBM = pl.BlockSpec(memory_space=pltpu.HBM)
ANY = pl.BlockSpec(memory_space=pl.ANY)

PRE, HEAD, CACHE = 4, 8, 4
STEPS = 3
SLOT = 4
ROWS = 16
GROUP = 8
HD = 128
BLK = 128
KS = 8
EPS = 1e-05
CHUNKS = 8
AHEAD = 4
TALL = 128
FIRST = 2
PEERS = (0, 2, 1, 3)
ORDER = (2, 1, 3)
HELD = 5


def hbm(array):
    return pltpu.with_memory_space_constraint(array, pltpu.HBM)


def vmem(array):
    return pltpu.with_memory_space_constraint(array, pltpu.VMEM)


def prefill_copies(start, x_hbm, w_hbm, x, w, x_sems, w_sems):
    depth = x.shape[2]

    def copies(k):
        lanes = pl.ds(pl.multiple_of((start + k) * depth, depth), depth)
        return [
            pltpu.make_async_copy(w_hbm.at[lanes, :], w.at[k], w_sems.at[k]),
            pltpu.make_async_copy(x_hbm.at[:, lanes], x.at[k], x_sems.at[k]),
        ]

    return copies


def prefill_steps(start, copies, gain, x, w, acc, squares):
    chunks, rows, depth = x.shape

    def step(k, carry):
        for copy in copies(k):
            copy.wait()

        @pl.when(k + AHEAD < chunks)
        def _():
            for copy in copies(k + AHEAD):
                copy.start()

        scale = gain[pl.ds(pl.multiple_of((start + k) * depth, depth), depth)].reshape(1, depth)
        for r in range(rows // TALL):
            at = slice(r * TALL, (r + 1) * TALL)
            part = squares[at, :]
            scaled = []
            for n in range(depth // 128):
                lanes = slice(n * 128, (n + 1) * 128)
                tile = x[k, at, lanes]
                floats = tile.astype(F32)
                part = part + floats * floats
                scaled.append(tile * scale[:, lanes])
            squares[at, :] = part
            acc[at, :] += jnp.dot(
                jnp.concatenate(scaled, axis=1), w[k], preferred_element_type=F32
            )
        return carry

    lax.fori_loop(0, chunks, step, 0)


def prefill_scratch(rows, width, cols, chunks):
    depth = width // CHUNKS
    return [
        pltpu.VMEM((chunks, rows, depth), BF16),
        pltpu.VMEM((chunks, depth, cols), BF16),
        pltpu.VMEM((width,), BF16),
        pltpu.SemaphoreType.DMA((chunks,)),
        pltpu.SemaphoreType.DMA((chunks,)),
        pltpu.SemaphoreType.DMA((1,)),
    ]


def begin_kernel(
    kept_hbm, live_hbm, kv_hbm, x_hbm, gain_hbm, w_hbm,
    kv, bias, acc, squares,
    kept, live, small, blocks, x, w, gain, x_sems, w_sems, gain_sem,
):
    first = pltpu.make_async_copy(kept_hbm, kept, small.at[0])
    second = pltpu.make_async_copy(live_hbm, live, small.at[1])
    third = pltpu.make_async_copy(gain_hbm, gain, gain_sem.at[0])
    first.start()
    second.start()
    third.start()
    copies = prefill_copies(0, x_hbm, w_hbm, x, w, x_sems, w_sems)
    for k in range(min(AHEAD, x.shape[0])):
        for copy in copies(k):
            copy.start()
    acc[...] = jnp.zeros_like(acc)
    squares[...] = jnp.zeros_like(squares)
    first.wait()
    arriving = []
    for i in range(PRE):
        for t in range(KS):
            copy = pltpu.make_async_copy(kv_hbm.at[i, 0, kept[i, t]], kv.at[i, t], blocks.at[i, t])
            copy.start()
            arriving.append(copy)
    second.wait()
    token = lax.broadcasted_iota(jnp.int32, (1, KS * BLK), 1)
    for i in range(PRE):
        bias[i : i + 1, :] = jnp.where(token < live[i] * BLK, 0.0, -1e30)
    third.wait()
    prefill_steps(0, copies, gain, x, w, acc, squares)
    for copy in arriving:
        copy.wait()


def begin(kept, live, kv, x, gain, w):
    rows, width = x.shape
    cols = w.shape[1]
    return pl.pallas_call(
        begin_kernel,
        in_specs=[HBM] * 6,
        out_specs=[VMEM] * 4,
        out_shape=[
            pltpu.VMEM((PRE, KS, BLK, 2 * HD), BF16),
            pltpu.VMEM((PRE, KS * BLK), F32),
            pltpu.VMEM((rows, cols), F32),
            pltpu.VMEM((rows, 128), F32),
        ],
        scratch_shapes=[
            pltpu.SMEM(kept.shape, jnp.int32),
            pltpu.SMEM(live.shape, jnp.int32),
            pltpu.SemaphoreType.DMA((2,)),
            pltpu.SemaphoreType.DMA((PRE, KS)),
            *prefill_scratch(rows, width, cols, FIRST),
        ],
        compiler_params=pltpu.CompilerParams(vmem_limit_bytes=16 * 1024 * 1024),
        cost_estimate=pl.CostEstimate(
            flops=2 * rows * width * cols * FIRST // CHUNKS,
            bytes_accessed=(2 << 20) + 2 * (rows + cols) * width * FIRST // CHUNKS,
            transcendentals=0,
        ),
        name="begin",
    )(hbm(kept), hbm(live), hbm(kv), hbm(x), hbm(gain), hbm(w))


def finish_kernel(
    x_hbm, gain_hbm, w_hbm, weight_hbm, before, before_squares, after_ref,
    out_ref, held,
    acc, squares, held_sem, x, w, gain, x_sems, w_sems, gain_sem,
):
    third = pltpu.make_async_copy(gain_hbm, gain, gain_sem.at[0])
    third.start()
    copies = prefill_copies(FIRST, x_hbm, w_hbm, x, w, x_sems, w_sems)
    for k in range(min(AHEAD, x.shape[0])):
        for copy in copies(k):
            copy.start()
    weight = pltpu.make_async_copy(weight_hbm.at[pl.ds(0, held.shape[0]), :], held, held_sem.at[0])
    weight.start()
    acc[...] = before[...]
    squares[...] = before_squares[...]
    third.wait()
    prefill_steps(FIRST, copies, gain, x, w, acc, squares)
    mean = jnp.sum(squares[...], axis=1, keepdims=True) * (1.0 / x_hbm.shape[1])
    out_ref[...] = (acc[...] * lax.rsqrt(mean + EPS)).astype(BF16)
    weight.wait()


def finish(x, gain, w, weight, before, before_squares, after):
    rows, width = x.shape
    cols = w.shape[1]
    return pl.pallas_call(
        finish_kernel,
        in_specs=[HBM] * 4 + [VMEM] * 2 + [ANY],
        out_specs=[VMEM] * 2,
        out_shape=[
            jax.ShapeDtypeStruct((rows, cols), BF16),
            pltpu.VMEM((weight.shape[0] * HELD // GROUP, weight.shape[1]), BF16),
        ],
        scratch_shapes=[
            pltpu.VMEM((rows, cols), F32),
            pltpu.VMEM((rows, 128), F32),
            pltpu.SemaphoreType.DMA((1,)),
            *prefill_scratch(rows, width, cols, CHUNKS - FIRST),
        ],
        compiler_params=pltpu.CompilerParams(vmem_limit_bytes=20 * 1024 * 1024),
        cost_estimate=pl.CostEstimate(
            flops=2 * rows * width * cols * (CHUNKS - FIRST) // CHUNKS,
            bytes_accessed=2 * (rows + cols) * width * (CHUNKS - FIRST) // CHUNKS,
            transcendentals=0,
        ),
        name="finish",
    )(hbm(x), hbm(gain), hbm(w), hbm(weight), vmem(before), vmem(before_squares), after)


def attend_kernel(q0, q1, q2, q3, kv, bias, out_ref, turned):
    mine = lax.axis_index("pre")
    group = lax.axis_index("cache")
    lane = lax.broadcasted_iota(jnp.int32, (GROUP, HD), 1)
    for k, q_ref in zip(PEERS, (q0, q1, q2, q3)):
        for s in range(STEPS):
            floats = q_ref[s].astype(F32)
            for j in range(GROUP):
                at = (k * STEPS + s) * CACHE * GROUP + j
                turned[pl.ds(at, CACHE, stride=GROUP), :] = floats[:, j * HD : (j + 1) * HD]
    scores = []
    for k in range(PRE):
        blocks = []
        for s in range(STEPS):
            at = (k * STEPS + s) * CACHE * GROUP + group * GROUP
            blocks.append(turned[pl.ds(pl.multiple_of(at, GROUP), GROUP), :])
        blocks.append(jnp.zeros((GROUP, HD), F32))
        q = jnp.concatenate(blocks, axis=0).astype(BF16)
        keys = kv[mine ^ k, :, :, :HD].reshape(KS * BLK, HD)
        scores.append(
            lax.dot_general(q, keys, (((1,), (1,)), ((), ())), preferred_element_type=F32)
        )
    tops, totals, terms = [], [], []
    for k in range(PRE):
        biased = scores[k] * (1.0 / math.sqrt(HD)) + bias[pl.ds(mine ^ k, 1), :]
        top = jnp.max(biased, axis=1, keepdims=True).astype(BF16).astype(F32)
        term = jnp.exp(biased - top)
        tops.append(top)
        totals.append(jnp.sum(term, axis=1, keepdims=True))
        terms.append(term.astype(BF16))
    for k in range(PRE):
        values = kv[mine ^ k, :, :, HD:].reshape(KS * BLK, HD)
        weighted = jnp.dot(terms[k], values, preferred_element_type=F32) / totals[k]
        high = totals[k].astype(BF16).astype(F32)
        low = totals[k] - high
        figures = jnp.zeros((GROUP, HD), F32)
        for s in range(STEPS):
            rows = slice(s * GROUP, (s + 1) * GROUP)
            figures = jnp.where(lane == s, tops[k][rows], figures)
            figures = jnp.where(lane == s + 4, high[rows], figures)
            figures = jnp.where(lane == s + 8, low[rows], figures)
        message = jnp.concatenate([weighted[: STEPS * GROUP], figures], axis=0).astype(BF16)
        for c in range(CACHE):
            out_ref[(mine ^ k) * CACHE + c] = message


def attend(queries, kv, bias):
    return pl.pallas_call(
        attend_kernel,
        in_specs=[VMEM] * 6,
        out_specs=VMEM,
        out_shape=pltpu.VMEM((PRE * CACHE, SLOT * GROUP, HD), BF16),
        scratch_shapes=[pltpu.VMEM((PRE * STEPS * CACHE * GROUP, HD), F32)],
        compiler_params=pltpu.CompilerParams(vmem_limit_bytes=4 * 1024 * 1024),
        cost_estimate=pl.CostEstimate(
            flops=2 * PRE * 2 * 32 * 1024 * 128, bytes_accessed=1 << 21, transcendentals=1 << 17
        ),
        name="attend",
    )(*queries, vmem(kv), vmem(bias))


def project_kernel(parts_ref, held, w_hbm, out_ref, sheet, w, sems):
    wide = HD * HEAD
    copies = []
    for j in range(HELD, GROUP):
        copies.append(
            pltpu.make_async_copy(
                w_hbm.at[pl.ds(j * wide, wide), :], w.at[j - HELD], sems.at[j - HELD]
            )
        )
        copies[-1].start()
    sheet[...] = jnp.zeros_like(sheet)
    for c in range(CACHE):
        parts = [parts_ref[p * CACHE + c].astype(F32) for p in range(PRE)]
        figures = [part[STEPS * GROUP :] for part in parts]
        for s in range(STEPS):
            tops = [f[:, s : s + 1] for f in figures]
            totals = [f[:, s + 4 : s + 5] + f[:, s + 8 : s + 9] for f in figures]
            top = functools.reduce(jnp.maximum, tops)
            shares = [jnp.exp(t - top) * total for t, total in zip(tops, totals)]
            scale = 1.0 / functools.reduce(jnp.add, shares)
            joined = functools.reduce(
                jnp.add,
                [
                    (share * scale) * part[s * GROUP : (s + 1) * GROUP]
                    for share, part in zip(shares, parts)
                ],
            )
            sheet[pl.ds(s * CACHE + c, GROUP, stride=ROWS), :] = joined
    spread = (
        lax.broadcasted_iota(jnp.int32, (HD, wide), 1) // HEAD
        == lax.broadcasted_iota(jnp.int32, (HD, wide), 0)
    ).astype(BF16)
    repeated = jnp.dot(
        sheet[...].astype(BF16), spread, preferred_element_type=F32
    ).astype(BF16)
    block = lax.broadcasted_iota(jnp.int32, (ROWS, wide), 1) % HEAD
    total = jnp.zeros((HEAD * ROWS, out_ref.shape[2]), F32)
    for j in range(GROUP):
        if j < HELD:
            weight = held[j * wide : (j + 1) * wide, :]
        else:
            copies[j - HELD].wait()
            weight = w[j - HELD]
        rows_j = repeated[j * ROWS : (j + 1) * ROWS, :]
        lhs = jnp.concatenate(
            [jnp.where(block == h, rows_j, jnp.zeros_like(rows_j)) for h in range(HEAD)], axis=0
        )
        total = total + jnp.dot(lhs, weight, preferred_element_type=F32)
    out_ref[...] = total.reshape(out_ref.shape).astype(BF16)


def project(parts, held, weight):
    cols = weight.shape[1]
    return pl.pallas_call(
        project_kernel,
        in_specs=[VMEM, VMEM, HBM],
        out_specs=VMEM,
        out_shape=pltpu.VMEM((HEAD, ROWS, cols), BF16),
        scratch_shapes=[
            pltpu.VMEM((GROUP * ROWS, HD), F32),
            pltpu.VMEM((GROUP - HELD, HD * HEAD, cols), BF16),
            pltpu.SemaphoreType.DMA((GROUP - HELD,)),
        ],
        compiler_params=pltpu.CompilerParams(vmem_limit_bytes=8 * 1024 * 1024),
        cost_estimate=pl.CostEstimate(
            flops=2 * 128 * 8192 * 256, bytes_accessed=1 << 22, transcendentals=0
        ),
        name="project",
    )(parts, vmem(held), hbm(weight))


def total_kernel(terms_ref, out_ref):
    total = jnp.sum(terms_ref[...].astype(F32), axis=0)
    for s in range(STEPS):
        out_ref[s] = total[s * CACHE : (s + 1) * CACHE].astype(BF16)


def total_of(terms):
    cols = terms.shape[2]
    return pl.pallas_call(
        total_kernel,
        in_specs=[VMEM],
        out_specs=VMEM,
        out_shape=jax.ShapeDtypeStruct((STEPS, CACHE, cols), BF16),
        compiler_params=pltpu.CompilerParams(vmem_limit_bytes=1024 * 1024),
        name="total",
    )(terms)


def body(prompt_kv, kept, live_count, queries, out_weight, prefill_x, prefill_gain, kv_weight):
    queries = queries.reshape(STEPS, CACHE, GROUP * HD)
    around = {0: queries}
    for k in ORDER:
        around[k] = lax.ppermute(queries, "pre", [(i, i ^ k) for i in range(PRE)])
    taken = (prefill_x, prefill_gain, kv_weight.reshape(8192, 256))
    kv, bias, *begun = begin(kept.reshape(PRE, KS), live_count.reshape(PRE), prompt_kv, *taken)
    parts = attend([around[k] for k in PEERS], kv, bias)
    sent = lax.all_to_all(parts, ("pre", "cache"), split_axis=0, concat_axis=0, tiled=True)
    weight = out_weight.reshape(8192, 256)
    next_kv, held = finish(*taken, weight, *begun, parts)
    terms = project(sent, held, weight)
    terms = lax.all_to_all(terms, "head", split_axis=0, concat_axis=0, tiled=True)
    attended = total_of(terms)
    return (attended.reshape(STEPS, CACHE, 1, 256), next_kv.reshape(512, 1, 256))


def solution(mesh):
    in_specs = (
        P("cache", "head", "pre", None, None),
        P("cache", "head", "pre", None),
        P("cache", "head"),
        P(None, None, "pre", "head"),
        P("head", None, "cache", None),
        P(("pre", "cache"), None),
        P(),
        P(None, "head", None),
    )
    out_specs = (P(None, None, "pre", ("head", "cache")), P(("pre", "cache"), "head", None))
    return jax.shard_map(body, mesh=mesh, in_specs=in_specs, out_specs=out_specs, check_vma=False)
```

time: 58.5 us -> 38.2 us (0.65)
  local copies, waits for them, and re-layouts: 13.9 us -> 0.01 us
  blocking collectives: 0 us -> 12 us
  waiting for transfers between devices: 10.7 us -> 1.07 us
  starting transfers between devices: 18 us -> 11.2 us
  Pallas kernels: 14.7 us -> 12.9 us
    unnamed x18 -> x2, local copies, waits for them, and re-layouts: 13.8 us -> 0.01 us
    all_to_all x0 -> x1, blocking collectives: none -> 12 us  [body(): lax.all_to_all(terms, 'head', split_axis=0, concat_axis=0, tiled=True)]
    all_to_all x1 -> x0, starting transfers between devices: 8.27 us -> none  [body(): lax.all_to_all(terms, 'head', split_axis=0, concat_axis=0, tiled=True)]
    all_to_all x1, waiting for transfers between devices: 6.65 us -> 0.52 us  [body(): lax.all_to_all(parts, ('pre', 'cache'), split_axis=0, concat_axis=0, tile...]
    ppermute x3, waiting for transfers between devices: 4.06 us -> 0.56 us  [body(): around[k] = lax.ppermute(queries, 'pre', [(i, i ^ k) for i in range(PRE)])]
    all_to_all x1, starting transfers between devices: 5.16 us -> 6.72 us  [body(): lax.all_to_all(parts, ('pre', 'cache'), split_axis=0, concat_axis=0, tile...]
    pallas_call x3 -> x4, Pallas kernels: 13.2 us -> 12.3 us  [the longest x1 6.24 us: finish(): pl.pallas_call(finish_kernel, in_specs=[HBM] * 4 + [VMEM] * 2 + [ANY], ou...]
    pallas_call x1, Pallas kernels: 1.45 us -> 0.61 us  [total_of(): pl.pallas_call(total_kernel, in_specs=[VMEM], out_specs=VMEM, out_shape=j...]
  transfers between devices with their start and end apart: 5 -> 4, of which waited for: 3 -> 2; matrix products, arithmetic and copies ran while one was open for 0% -> 0% of each run, Pallas kernels for 9% -> 24%
where the time goes in v2:
time: 38.2 us; the launch traced here: 37.9 us
  Pallas kernels  12.9 us (34%)
  blocking collectives  12 us (31%)
  starting transfers between devices  11.2 us (29%)
  waiting for transfers between devices  1.07 us (3%)
  between operations  0.68 us (2%)
    all_to_all x1, blocking collectives, body(): lax.all_to_all(terms, 'head', split_axis=0, concat_axis=0, tiled=True)  12 us
    all_to_all x1, starting transfers between devices, body(): lax.all_to_all(parts, ('pre', 'cache'), split_axis=0, concat_axis=0, tile...  6.72 us
    pallas_call x1, Pallas kernels, finish(): pl.pallas_call(finish_kernel, in_specs=[HBM] * 4 + [VMEM] * 2 + [ANY], ou...  6.24 us
    ppermute x3, starting transfers between devices, body(): around[k] = lax.ppermute(queries, 'pre', [(i, i ^ k) for i in range(PRE)])  4.52 us
    pallas_call x1, Pallas kernels, begin(): pl.pallas_call(begin_kernel, in_specs=[HBM] * 6, out_specs=[VMEM] * 4, ou...  2.96 us
    pallas_call x1, Pallas kernels, project(): pl.pallas_call(project_kernel, in_specs=[VMEM, VMEM, HBM], out_specs=VMEM...  1.69 us
    pallas_call x1, Pallas kernels, attend(): pl.pallas_call(attend_kernel, in_specs=[VMEM] * 6, out_specs=VMEM, out_sh...  1.41 us
  transfers between devices with their start and end apart: 4, of which 2 were waited for; matrix products, arithmetic and copies ran while one was open for 0% of the time, Pallas kernels for 24%

profile of v2, /device:TPU:1, one launch (start us, length us, event | category | flops | bytes accessed | tf_op | source)
XLA Modules:
  0.0 37.9 jit_solution(2328908404360717895)
XLA Ops:
  0.6 3.7 %collective-permute-start = (bf16[3,4,1024]{2,1,0:T(4,128)(2,1)}, bf16[3,4,1024]{2,1,0:T(4,128)(2,1)S(1)}, u32[]{:S(2)}, u32[]{:S(2)}) collective-permute-start(bf16[3,4,1024]{2,1,0:T(4,128)(2,1)} %bitcast.9), channel_id=1, source_target_pairs={{0,64},{32,96},{64,0},{96,32},{1,65},{33,97},{65,1},{97,33},{2,66}... | collective-permute-start | bytes 73736 | tf_op jit(solution)/shard_map/ppermute | solution.py:368
  4.3 0.3 collective-permute-start.1
  4.6 0.6 %collective-permute-start.2 = (bf16[3,4,1024]{2,1,0:T(4,128)(2,1)}, bf16[3,4,1024]{2,1,0:T(4,128)(2,1)S(1)}, u32[]{:S(2)}, u32[]{:S(2)}) collective-permute-start(bf16[3,4,1024]{2,1,0:T(4,128)(2,1)} %bitcast.11), channel_id=1, source_target_pairs={{0,96},{32,64},{64,32},{96,0},{1,97},{33,65},{65,33},{97,1},{2,98}... | collective-permute-start | bytes 73736 | tf_op jit(solution)/shard_map/ppermute | solution.py:368
  5.1 0.0 copy-start
  5.1 3.0 %begin.1 = (bf16[4,8,128,256]{3,2,1,0:T(8,128)(2,1)S(1)}, f32[4,1024]{1,0:T(4,128)S(1)}, f32[512,256]{1,0:T(8,128)S(1)}, f32[512,128]{1,0:T(8,128)S(1)}) custom-call(s32[4,8]{1,0:T(4,128)} %bitcast.18, s32[4]{0:T(128)} %bitcast.19, bf16[4,1,32,128,256]{4,3,2,1,0:T(8,128)(2,1)} %kv_hbm.1, bf16[512,8192]{1,0:T(8,128)(2,1)} %x_hbm.3, bf16[8192]{0:T(1024)(128)(2,1)} %gain_hbm.3, ...), custom_call_target="tpu_custom_call" | custom-call | flops 536870912 | bytes 5242880 | tf_op jit(solution)/shard_map/begin/pallas_call | solution.py:138
  8.1 0.0 collective-permute-done.q1
  8.1 0.0 collective-permute-done.1.q2
  8.1 0.6 %collective-permute-done.2.q3 = bf16[3,4,1024]{2,1,0:T(4,128)(2,1)S(1)} collective-permute-done((bf16[3,4,1024]{2,1,0:T(4,128)(2,1)}, bf16[3,4,1024]{2,1,0:T(4,128)(2,1)S(1)}, u32[]{:S(2)}, u32[]{:S(2)}) %collective-permute-start.2) | collective-permute-done | bytes 24608 | tf_op jit(solution)/shard_map/ppermute | solution.py:368
  8.7 0.0 copy-done
  8.7 1.4 %attend.1.after_ref = bf16[16,32,128]{2,1,0:T(8,128)(2,1)} custom-call(bf16[3,4,1024]{2,1,0:T(4,128)(2,1)S(1)} %bitcast.12, bf16[3,4,1024]{2,1,0:T(4,128)(2,1)S(1)} %collective-permute-done.q1, bf16[3,4,1024]{2,1,0:T(4,128)(2,1)S(1)} %collective-permute-done.1.q2, bf16[3,4,1024]{2,1,0:T(4,128)(2,1)S(1)} %collective-permute-done.2.q3, ...), custom_call_target="tpu_custom_call" | custom-call | flops 67108864 | bytes 2097152 | tf_op jit(solution)/shard_map/attend/pallas_call | solution.py:261
  10.1 6.7 %all-to-all-start = ((bf16[16,32,128]{2,1,0:T(8,128)(2,1)}), bf16[16,32,128]{2,1,0:T(8,128)(2,1)S(1)}, u32[]{:S(2)}, u32[]{:S(2)}) async-start(bf16[16,32,128]{2,1,0:T(8,128)(2,1)} %attend.1.after_ref), calls=%async_computation | async-start | bytes 262144 | tf_op jit(solution)/shard_map/all_to_all | solution.py:372
  16.8 6.2 %finish.1 = (bf16[512,256]{1,0:T(8,128)(2,1)}, bf16[5120,256]{1,0:T(8,128)(2,1)S(1)}) custom-call(bf16[512,8192]{1,0:T(8,128)(2,1)} %x_hbm.3, bf16[8192]{0:T(1024)(128)(2,1)} %gain_hbm.3, bf16[8192,256]{1,0:T(8,128)(2,1)} %bitcast.16, bf16[8192,256]{1,0:T(8,128)(2,1)} %bitcast.13, f32[512,256]{1,0:T(8,128)S(1)} %get-tuple-element.10.before, ...), custom_call_target="tpu_custom_call" | custom-call | flops 1610612736 | bytes 9437184 | tf_op jit(solution)/shard_map/finish/pallas_call | solution.py:190
  23.1 0.5 %all-to-all-done.parts_ref = bf16[16,32,128]{2,1,0:T(8,128)(2,1)S(1)} async-done(((bf16[16,32,128]{2,1,0:T(8,128)(2,1)}), bf16[16,32,128]{2,1,0:T(8,128)(2,1)S(1)}, u32[]{:S(2)}, u32[]{:S(2)}) %all-to-all-start) | async-done | bytes 131104 | tf_op jit(solution)/shard_map/all_to_all | solution.py:372
  23.6 1.7 %project.1 = bf16[8,16,256]{2,1,0:T(8,128)(2,1)S(1)} custom-call(bf16[16,32,128]{2,1,0:T(8,128)(2,1)S(1)} %all-to-all-done.parts_ref, bf16[5120,256]{1,0:T(8,128)(2,1)S(1)} %get-tuple-element.12.held, bf16[8192,256]{1,0:T(8,128)(2,1)} %bitcast.14), custom_call_target="tpu_custom_call" | custom-call | flops 536870912 | bytes 4194304 | tf_op jit(solution)/shard_map/project/pallas_call | solution.py:328
  25.3 12.0 %all_to_all.10.terms_ref = bf16[8,16,256]{2,1,0:T(8,128)(2,1)S(1)} all-to-all(bf16[8,16,256]{2,1,0:T(8,128)(2,1)S(1)} %project.1), channel_id=1, replica_groups=mesh['pre'=4,'head'=8,'cache'=4] {'head'}, dimensions={0} | all-to-all | bytes 131072 | tf_op jit(solution)/shard_map/all_to_all | solution.py:376
  37.3 0.6 %total.1 = bf16[3,4,256]{2,1,0:T(4,128)(2,1)} custom-call(bf16[8,16,256]{2,1,0:T(8,128)(2,1)S(1)} %all_to_all.10.terms_ref), custom_call_target="tpu_custom_call" | custom-call | tf_op jit(solution)/shard_map/total/pallas_call | solution.py:354
Async XLA Ops:
  0.6 7.5 %collective-permute-start = (bf16[3,4,1024]{2,1,0:T(4,128)(2,1)}, bf16[3,4,1024]{2,1,0:T(4,128)(2,1)S(1)}, u32[]{:S(2)}, u32[]{:S(2)}) collective-permute-start(bf16[3,4,1024]{2,1,0:T(4,128)(2,1)} %bitcast.9), channel_id=1, source_target_pairs={{0,64},{32,96},{64,0},{96,32},{1,65},{33,97},{65,1},{97,33},{2,66}... | collective-permute-start | bytes 73736 | tf_op jit(solution)/shard_map/ppermute | solution.py:368
  4.3 3.9 %collective-permute-start.1 = (bf16[3,4,1024]{2,1,0:T(4,128)(2,1)}, bf16[3,4,1024]{2,1,0:T(4,128)(2,1)S(1)}, u32[]{:S(2)}, u32[]{:S(2)}) collective-permute-start(bf16[3,4,1024]{2,1,0:T(4,128)(2,1)} %bitcast.10), channel_id=1, source_target_pairs={{0,32},{32,0},{64,96},{96,64},{1,33},{33,1},{65,97},{97,65},{2,34}... | collective-permute-start | bytes 73736 | tf_op jit(solution)/shard_map/ppermute | solution.py:368
  4.6 4.1 %collective-permute-start.2 = (bf16[3,4,1024]{2,1,0:T(4,128)(2,1)}, bf16[3,4,1024]{2,1,0:T(4,128)(2,1)S(1)}, u32[]{:S(2)}, u32[]{:S(2)}) collective-permute-start(bf16[3,4,1024]{2,1,0:T(4,128)(2,1)} %bitcast.11), channel_id=1, source_target_pairs={{0,96},{32,64},{64,32},{96,0},{1,97},{33,65},{65,33},{97,1},{2,98}... | collective-permute-start | bytes 73736 | tf_op jit(solution)/shard_map/ppermute | solution.py:368
  5.1 3.5 %copy-start = (bf16[3,4,1,1024]{3,1,2,0:T(4,128)(2,1)S(1)}, bf16[3,4,1,1024]{3,1,2,0:T(4,128)(2,1)}, u32[]{:S(2)}) copy-start(bf16[3,4,1,1024]{3,1,2,0:T(4,128)(2,1)} %param.11) | copy-start | bytes 73732
  10.1 13.5 %all-to-all-start = ((bf16[16,32,128]{2,1,0:T(8,128)(2,1)}), bf16[16,32,128]{2,1,0:T(8,128)(2,1)S(1)}, u32[]{:S(2)}, u32[]{:S(2)}) async-start(bf16[16,32,128]{2,1,0:T(8,128)(2,1)} %attend.1.after_ref), calls=%async_computation | async-start | bytes 262144 | tf_op jit(solution)/shard_map/all_to_all | solution.py:372

commit v3 on v2

--- a/solution.py
+++ b/solution.py
@@ -25,12 +25,10 @@
 KS = 8
 EPS = 1e-05
 CHUNKS = 8
-AHEAD = 4
+AHEAD = 3
 TALL = 128
-FIRST = 2
-PEERS = (0, 2, 1, 3)
-ORDER = (2, 1, 3)
-HELD = 5
+PEERS = (0, 1, 2, 3)
+HELD = 6
 
 
 def hbm(array):
@@ -41,11 +39,11 @@
     return pltpu.with_memory_space_constraint(array, pltpu.VMEM)
 
 
-def prefill_copies(start, x_hbm, w_hbm, x, w, x_sems, w_sems):
+def prefill_copies(x_hbm, w_hbm, x, w, x_sems, w_sems):
     depth = x.shape[2]
 
     def copies(k):
-        lanes = pl.ds(pl.multiple_of((start + k) * depth, depth), depth)
+        lanes = pl.ds(pl.multiple_of(k * depth, depth), depth)
         return [
             pltpu.make_async_copy(w_hbm.at[lanes, :], w.at[k], w_sems.at[k]),
             pltpu.make_async_copy(x_hbm.at[:, lanes], x.at[k], x_sems.at[k]),
@@ -54,7 +52,7 @@
     return copies
 
 
-def prefill_steps(start, copies, gain, x, w, acc, squares):
+def prefill_steps(copies, gain, x, w, acc, squares, weight):
     chunks, rows, depth = x.shape
 
     def step(k, carry):
@@ -66,7 +64,11 @@
             for copy in copies(k + AHEAD):
                 copy.start()
 
-        scale = gain[pl.ds(pl.multiple_of((start + k) * depth, depth), depth)].reshape(1, depth)
+        @pl.when(k == 4)
+        def _():
+            weight.start()
+
+        scale = gain[pl.ds(pl.multiple_of(k * depth, depth), depth)].reshape(1, depth)
         for r in range(rows // TALL):
             at = slice(r * TALL, (r + 1) * TALL)
             part = squares[at, :]
@@ -86,35 +88,11 @@
     lax.fori_loop(0, chunks, step, 0)
 
 
-def prefill_scratch(rows, width, cols, chunks):
-    depth = width // CHUNKS
-    return [
-        pltpu.VMEM((chunks, rows, depth), BF16),
-        pltpu.VMEM((chunks, depth, cols), BF16),
-        pltpu.VMEM((width,), BF16),
-        pltpu.SemaphoreType.DMA((chunks,)),
-        pltpu.SemaphoreType.DMA((chunks,)),
-        pltpu.SemaphoreType.DMA((1,)),
-    ]
-
-
-def begin_kernel(
-    kept_hbm, live_hbm, kv_hbm, x_hbm, gain_hbm, w_hbm,
-    kv, bias, acc, squares,
-    kept, live, small, blocks, x, w, gain, x_sems, w_sems, gain_sem,
-):
+def load_kernel(kept_hbm, live_hbm, kv_hbm, kv, bias, kept, live, small, blocks):
     first = pltpu.make_async_copy(kept_hbm, kept, small.at[0])
     second = pltpu.make_async_copy(live_hbm, live, small.at[1])
-    third = pltpu.make_async_copy(gain_hbm, gain, gain_sem.at[0])
     first.start()
     second.start()
-    third.start()
-    copies = prefill_copies(0, x_hbm, w_hbm, x, w, x_sems, w_sems)
-    for k in range(min(AHEAD, x.shape[0])):
-        for copy in copies(k):
-            copy.start()
-    acc[...] = jnp.zeros_like(acc)
-    squares[...] = jnp.zeros_like(squares)
     first.wait()
     arriving = []
     for i in range(PRE):
@@ -126,70 +104,59 @@
     token = lax.broadcasted_iota(jnp.int32, (1, KS * BLK), 1)
     for i in range(PRE):
         bias[i : i + 1, :] = jnp.where(token < live[i] * BLK, 0.0, -1e30)
-    third.wait()
-    prefill_steps(0, copies, gain, x, w, acc, squares)
     for copy in arriving:
         copy.wait()
 
 
-def begin(kept, live, kv, x, gain, w):
-    rows, width = x.shape
-    cols = w.shape[1]
-    return pl.pallas_call(
-        begin_kernel,
-        in_specs=[HBM] * 6,
-        out_specs=[VMEM] * 4,
+def load(kept, live, kv):
+    return pl.pallas_call(
+        load_kernel,
+        in_specs=[HBM] * 3,
+        out_specs=[VMEM] * 2,
         out_shape=[
             pltpu.VMEM((PRE, KS, BLK, 2 * HD), BF16),
             pltpu.VMEM((PRE, KS * BLK), F32),
-            pltpu.VMEM((rows, cols), F32),
-            pltpu.VMEM((rows, 128), F32),
         ],
         scratch_shapes=[
             pltpu.SMEM(kept.shape, jnp.int32),
             pltpu.SMEM(live.shape, jnp.int32),
             pltpu.SemaphoreType.DMA((2,)),
             pltpu.SemaphoreType.DMA((PRE, KS)),
-            *prefill_scratch(rows, width, cols, FIRST),
-        ],
-        compiler_params=pltpu.CompilerParams(vmem_limit_bytes=16 * 1024 * 1024),
-        cost_estimate=pl.CostEstimate(
-            flops=2 * rows * width * cols * FIRST // CHUNKS,
-            bytes_accessed=(2 << 20) + 2 * (rows + cols) * width * FIRST // CHUNKS,
-            transcendentals=0,
-        ),
-        name="begin",
-    )(hbm(kept), hbm(live), hbm(kv), hbm(x), hbm(gain), hbm(w))
-
-
-def finish_kernel(
-    x_hbm, gain_hbm, w_hbm, weight_hbm, before, before_squares, after_ref,
+        ],
+        compiler_params=pltpu.CompilerParams(vmem_limit_bytes=1024 * 1024),
+        cost_estimate=pl.CostEstimate(flops=0, bytes_accessed=2 << 20, transcendentals=0),
+        name="load",
+    )(hbm(kept), hbm(live), hbm(kv))
+
+
+def prefill_kernel(
+    x_hbm, gain_hbm, w_hbm, weight_hbm, after_ref,
     out_ref, held,
-    acc, squares, held_sem, x, w, gain, x_sems, w_sems, gain_sem,
+    acc, squares, x, w, gain, x_sems, w_sems, sems,
 ):
-    third = pltpu.make_async_copy(gain_hbm, gain, gain_sem.at[0])
+    third = pltpu.make_async_copy(gain_hbm, gain, sems.at[0])
     third.start()
-    copies = prefill_copies(FIRST, x_hbm, w_hbm, x, w, x_sems, w_sems)
-    for k in range(min(AHEAD, x.shape[0])):
+    copies = prefill_copies(x_hbm, w_hbm, x, w, x_sems, w_sems)
+    for k in range(AHEAD):
         for copy in copies(k):
             copy.start()
-    weight = pltpu.make_async_copy(weight_hbm.at[pl.ds(0, held.shape[0]), :], held, held_sem.at[0])
-    weight.start()
-    acc[...] = before[...]
-    squares[...] = before_squares[...]
+    weight = pltpu.make_async_copy(weight_hbm.at[pl.ds(0, held.shape[0]), :], held, sems.at[1])
+    acc[...] = jnp.zeros_like(acc)
+    squares[...] = jnp.zeros_like(squares)
     third.wait()
-    prefill_steps(FIRST, copies, gain, x, w, acc, squares)
+    prefill_steps(copies, gain, x, w, acc, squares, weight)
     mean = jnp.sum(squares[...], axis=1, keepdims=True) * (1.0 / x_hbm.shape[1])
     out_ref[...] = (acc[...] * lax.rsqrt(mean + EPS)).astype(BF16)
     weight.wait()
 
 
-def finish(x, gain, w, weight, before, before_squares, after):
+def prefill(x, gain, w, weight, after):
     rows, width = x.shape
     cols = w.shape[1]
-    return pl.pallas_call(
-        finish_kernel,
-        in_specs=[HBM] * 4 + [VMEM] * 2 + [ANY],
+    depth = width // CHUNKS
+    return pl.pallas_call(
+        prefill_kernel,
+        in_specs=[HBM] * 4 + [ANY],
         out_specs=[VMEM] * 2,
         out_shape=[
             jax.ShapeDtypeStruct((rows, cols), BF16),
@@ -198,17 +165,21 @@
         scratch_shapes=[
             pltpu.VMEM((rows, cols), F32),
             pltpu.VMEM((rows, 128), F32),
-            pltpu.SemaphoreType.DMA((1,)),
-            *prefill_scratch(rows, width, cols, CHUNKS - FIRST),
+            pltpu.VMEM((CHUNKS, rows, depth), BF16),
+            pltpu.VMEM((CHUNKS, depth, cols), BF16),
+            pltpu.VMEM((width,), BF16),
+            pltpu.SemaphoreType.DMA((CHUNKS,)),
+            pltpu.SemaphoreType.DMA((CHUNKS,)),
+            pltpu.SemaphoreType.DMA((2,)),
         ],
         compiler_params=pltpu.CompilerParams(vmem_limit_bytes=20 * 1024 * 1024),
         cost_estimate=pl.CostEstimate(
-            flops=2 * rows * width * cols * (CHUNKS - FIRST) // CHUNKS,
-            bytes_accessed=2 * (rows + cols) * width * (CHUNKS - FIRST) // CHUNKS,
+            flops=2 * rows * width * cols,
+            bytes_accessed=2 * (rows + cols) * width,
             transcendentals=0,
         ),
-        name="finish",
-    )(hbm(x), hbm(gain), hbm(w), hbm(weight), vmem(before), vmem(before_squares), after)
+        name="prefill",
+    )(hbm(x), hbm(gain), hbm(w), hbm(weight), after)
 
 
 def attend_kernel(q0, q1, q2, q3, kv, bias, out_ref, turned):
@@ -364,14 +335,15 @@
 def body(prompt_kv, kept, live_count, queries, out_weight, prefill_x, prefill_gain, kv_weight):
     queries = queries.reshape(STEPS, CACHE, GROUP * HD)
     around = {0: queries}
-    for k in ORDER:
+    for k in PEERS[1:]:
         around[k] = lax.ppermute(queries, "pre", [(i, i ^ k) for i in range(PRE)])
-    taken = (prefill_x, prefill_gain, kv_weight.reshape(8192, 256))
-    kv, bias, *begun = begin(kept.reshape(PRE, KS), live_count.reshape(PRE), prompt_kv, *taken)
+    kv, bias = load(kept.reshape(PRE, KS), live_count.reshape(PRE), prompt_kv)
     parts = attend([around[k] for k in PEERS], kv, bias)
     sent = lax.all_to_all(parts, ("pre", "cache"), split_axis=0, concat_axis=0, tiled=True)
     weight = out_weight.reshape(8192, 256)
-    next_kv, held = finish(*taken, weight, *begun, parts)
+    next_kv, held = prefill(
+        prefill_x, prefill_gain, kv_weight.reshape(8192, 256), weight, parts
+    )
     terms = project(sent, held, weight)
     terms = lax.all_to_all(terms, "head", split_axis=0, concat_axis=0, tiled=True)
     attended = total_of(terms)

time: 38.2 us -> 38.3 us (level)
  Pallas kernels: 12.9 us -> 13.4 us
  starting transfers between devices: 11.2 us -> 10.8 us
    pallas_call x2, Pallas kernels: 9.2 us -> 9.86 us  [the longest x1 7.18 us: prefill(): pl.pallas_call(prefill_kernel, in_specs=[HBM] * 4 + [ANY], out_specs=[VME...]
    all_to_all x1, waiting for transfers between devices: 0.52 us -> 0.01 us  [body(): lax.all_to_all(parts, ('pre', 'cache'), split_axis=0, concat_axis=0, tile...]
    ppermute x3, waiting for transfers between devices: 0.56 us -> 1.03 us  [body(): around[k] = lax.ppermute(queries, 'pre', [(i, i ^ k) for i in range(PRE)])]
    ppermute x3, starting transfers between devices: 4.52 us -> 4.06 us  [body(): around[k] = lax.ppermute(queries, 'pre', [(i, i ^ k) for i in range(PRE)])]
  transfers between devices with their start and end apart: 4 -> 4, of which waited for: 2 -> 1; matrix products, arithmetic and copies ran while one was open for 0% -> 0% of each run, Pallas kernels for 24% -> 26%
where the time goes in v3:
time: 38.3 us; the launch traced here: 37.9 us
  Pallas kernels  13.4 us (35%)
  blocking collectives  12 us (31%)
  starting transfers between devices  10.8 us (28%)
  waiting for transfers between devices  1.03 us (3%)
  between operations  0.68 us (2%)
    all_to_all x1, blocking collectives, body(): lax.all_to_all(terms, 'head', split_axis=0, concat_axis=0, tiled=True)  12 us
    pallas_call x1, Pallas kernels, prefill(): pl.pallas_call(prefill_kernel, in_specs=[HBM] * 4 + [ANY], out_specs=[VME...  7.18 us
    all_to_all x1, starting transfers between devices, body(): lax.all_to_all(parts, ('pre', 'cache'), split_axis=0, concat_axis=0, tile...  6.71 us
    ppermute x3, starting transfers between devices, body(): around[k] = lax.ppermute(queries, 'pre', [(i, i ^ k) for i in range(PRE)])  4.06 us
    pallas_call x1, Pallas kernels, load(): pl.pallas_call(load_kernel, in_specs=[HBM] * 3, out_specs=[VMEM] * 2, out...  2.68 us
    pallas_call x1, Pallas kernels, project(): pl.pallas_call(project_kernel, in_specs=[VMEM, VMEM, HBM], out_specs=VMEM...  1.52 us
    pallas_call x1, Pallas kernels, attend(): pl.pallas_call(attend_kernel, in_specs=[VMEM] * 6, out_specs=VMEM, out_sh...  1.41 us
    ppermute x3, waiting for transfers between devices, body(): around[k] = lax.ppermute(queries, 'pre', [(i, i ^ k) for i in range(PRE)])  1.03 us
  transfers between devices with their start and end apart: 4, of which 1 were waited for; matrix products, arithmetic and copies ran while one was open for 0% of the time, Pallas kernels for 26%

profile of v3, /device:TPU:1, one launch (start us, length us, event | category | flops | bytes accessed | tf_op | source)
XLA Modules:
  0.0 37.9 jit_solution(18091849422827436539)
XLA Ops:
  0.6 3.4 %collective-permute-start.2 = (bf16[3,4,1024]{2,1,0:T(4,128)(2,1)}, bf16[3,4,1024]{2,1,0:T(4,128)(2,1)S(1)}, u32[]{:S(2)}, u32[]{:S(2)}) collective-permute-start(bf16[3,4,1024]{2,1,0:T(4,128)(2,1)} %bitcast.9), channel_id=1, source_target_pairs={{0,96},{32,64},{64,32},{96,0},{1,97},{33,65},{65,33},{97,1},{2,98}... | collective-permute-start | bytes 73736 | tf_op jit(solution)/shard_map/ppermute | solution.py:339
  4.0 0.5 %collective-permute-start.1 = (bf16[3,4,1024]{2,1,0:T(4,128)(2,1)}, bf16[3,4,1024]{2,1,0:T(4,128)(2,1)S(1)}, u32[]{:S(2)}, u32[]{:S(2)}) collective-permute-start(bf16[3,4,1024]{2,1,0:T(4,128)(2,1)} %bitcast.10), channel_id=1, source_target_pairs={{0,64},{32,96},{64,0},{96,32},{1,65},{33,97},{65,1},{97,33},{2,66}... | collective-permute-start | bytes 73736 | tf_op jit(solution)/shard_map/ppermute | solution.py:339
  4.5 0.1 collective-permute-start
  4.7 0.0 copy-start
  4.7 2.7 %load.1 = (bf16[4,8,128,256]{3,2,1,0:T(8,128)(2,1)S(1)}, f32[4,1024]{1,0:T(4,128)S(1)}) custom-call(s32[4,8]{1,0:T(4,128)} %bitcast.17, s32[4]{0:T(128)} %bitcast.18, bf16[4,1,32,128,256]{4,3,2,1,0:T(8,128)(2,1)} %kv_hbm.1), custom_call_target="tpu_custom_call" | custom-call | bytes 2097152 | tf_op jit(solution)/shard_map/load/pallas_call | solution.py:112
  7.4 0.0 collective-permute-done.2.q3
  7.4 1.0 %collective-permute-done.1.q2 = bf16[3,4,1024]{2,1,0:T(4,128)(2,1)S(1)} collective-permute-done((bf16[3,4,1024]{2,1,0:T(4,128)(2,1)}, bf16[3,4,1024]{2,1,0:T(4,128)(2,1)S(1)}, u32[]{:S(2)}, u32[]{:S(2)}) %collective-permute-start.1) | collective-permute-done | bytes 24608 | tf_op jit(solution)/shard_map/ppermute | solution.py:339
  8.4 0.0 collective-permute-done.q1
  8.4 0.0 copy-done
  8.4 1.4 %attend.1.after_ref = bf16[16,32,128]{2,1,0:T(8,128)(2,1)} custom-call(bf16[3,4,1024]{2,1,0:T(4,128)(2,1)S(1)} %bitcast.12, bf16[3,4,1024]{2,1,0:T(4,128)(2,1)S(1)} %collective-permute-done.q1, bf16[3,4,1024]{2,1,0:T(4,128)(2,1)S(1)} %collective-permute-done.1.q2, bf16[3,4,1024]{2,1,0:T(4,128)(2,1)S(1)} %collective-permute-done.2.q3, ...), custom_call_target="tpu_custom_call" | custom-call | flops 67108864 | bytes 2097152 | tf_op jit(solution)/shard_map/attend/pallas_call | solution.py:232
  9.8 6.7 %all-to-all-start = ((bf16[16,32,128]{2,1,0:T(8,128)(2,1)}), bf16[16,32,128]{2,1,0:T(8,128)(2,1)S(1)}, u32[]{:S(2)}, u32[]{:S(2)}) async-start(bf16[16,32,128]{2,1,0:T(8,128)(2,1)} %attend.1.after_ref), calls=%async_computation | async-start | bytes 262144 | tf_op jit(solution)/shard_map/all_to_all | solution.py:342
  16.5 7.2 %prefill.1 = (bf16[512,256]{1,0:T(8,128)(2,1)}, bf16[6144,256]{1,0:T(8,128)(2,1)S(1)}) custom-call(bf16[512,8192]{1,0:T(8,128)(2,1)} %x_hbm.1, bf16[8192]{0:T(1024)(128)(2,1)} %gain_hbm.1, bf16[8192,256]{1,0:T(8,128)(2,1)} %bitcast.15, bf16[8192,256]{1,0:T(8,128)(2,1)} %bitcast.13, bf16[16,32,128]{2,1,0:T(8,128)(2,1)} %attend.1.after_ref), custom_call_target="tpu_custom_call" | custom-call | flops 2147483648 | bytes 12582912 | tf_op jit(solution)/shard_map/prefill/pallas_call | solution.py:157
  23.7 0.0 all-to-all-done.parts_ref
  23.7 1.5 %project.1 = bf16[8,16,256]{2,1,0:T(8,128)(2,1)S(1)} custom-call(bf16[16,32,128]{2,1,0:T(8,128)(2,1)S(1)} %all-to-all-done.parts_ref, bf16[6144,256]{1,0:T(8,128)(2,1)S(1)} %get-tuple-element.8.held, bf16[8192,256]{1,0:T(8,128)(2,1)} %bitcast.14), custom_call_target="tpu_custom_call" | custom-call | flops 536870912 | bytes 4194304 | tf_op jit(solution)/shard_map/project/pallas_call | solution.py:299
  25.3 12.0 %all_to_all.10.terms_ref = bf16[8,16,256]{2,1,0:T(8,128)(2,1)S(1)} all-to-all(bf16[8,16,256]{2,1,0:T(8,128)(2,1)S(1)} %project.1), channel_id=1, replica_groups=mesh['pre'=4,'head'=8,'cache'=4] {'head'}, dimensions={0} | all-to-all | bytes 131072 | tf_op jit(solution)/shard_map/all_to_all | solution.py:348
  37.3 0.6 %total.1 = bf16[3,4,256]{2,1,0:T(4,128)(2,1)} custom-call(bf16[8,16,256]{2,1,0:T(8,128)(2,1)S(1)} %all_to_all.10.terms_ref), custom_call_target="tpu_custom_call" | custom-call | tf_op jit(solution)/shard_map/total/pallas_call | solution.py:325
Async XLA Ops:
  0.6 6.8 %collective-permute-start.2 = (bf16[3,4,1024]{2,1,0:T(4,128)(2,1)}, bf16[3,4,1024]{2,1,0:T(4,128)(2,1)S(1)}, u32[]{:S(2)}, u32[]{:S(2)}) collective-permute-start(bf16[3,4,1024]{2,1,0:T(4,128)(2,1)} %bitcast.9), channel_id=1, source_target_pairs={{0,96},{32,64},{64,32},{96,0},{1,97},{33,65},{65,33},{97,1},{2,98}... | collective-permute-start | bytes 73736 | tf_op jit(solution)/shard_map/ppermute | solution.py:339
  4.0 4.4 %collective-permute-start.1 = (bf16[3,4,1024]{2,1,0:T(4,128)(2,1)}, bf16[3,4,1024]{2,1,0:T(4,128)(2,1)S(1)}, u32[]{:S(2)}, u32[]{:S(2)}) collective-permute-start(bf16[3,4,1024]{2,1,0:T(4,128)(2,1)} %bitcast.10), channel_id=1, source_target_pairs={{0,64},{32,96},{64,0},{96,32},{1,65},{33,97},{65,1},{97,33},{2,66}... | collective-permute-start | bytes 73736 | tf_op jit(solution)/shard_map/ppermute | solution.py:339
  4.5 3.9 %collective-permute-start = (bf16[3,4,1024]{2,1,0:T(4,128)(2,1)}, bf16[3,4,1024]{2,1,0:T(4,128)(2,1)S(1)}, u32[]{:S(2)}, u32[]{:S(2)}) collective-permute-start(bf16[3,4,1024]{2,1,0:T(4,128)(2,1)} %bitcast.11), channel_id=1, source_target_pairs={{0,32},{32,0},{64,96},{96,64},{1,33},{33,1},{65,97},{97,65},{2,34}... | collective-permute-start | bytes 73736 | tf_op jit(solution)/shard_map/ppermute | solution.py:339
  4.7 3.7 %copy-start = (bf16[3,4,1,1024]{3,1,2,0:T(4,128)(2,1)S(1)}, bf16[3,4,1,1024]{3,1,2,0:T(4,128)(2,1)}, u32[]{:S(2)}) copy-start(bf16[3,4,1,1024]{3,1,2,0:T(4,128)(2,1)} %param.11) | copy-start | bytes 73732
  9.8 13.9 %all-to-all-start = ((bf16[16,32,128]{2,1,0:T(8,128)(2,1)}), bf16[16,32,128]{2,1,0:T(8,128)(2,1)S(1)}, u32[]{:S(2)}, u32[]{:S(2)}) async-start(bf16[16,32,128]{2,1,0:T(8,128)(2,1)} %attend.1.after_ref), calls=%async_computation | async-start | bytes 262144 | tf_op jit(solution)/shard_map/all_to_all | solution.py:342

commit v4 on v2

--- a/solution.py
+++ b/solution.py
@@ -28,6 +28,7 @@
 AHEAD = 4
 TALL = 128
 FIRST = 2
+TURNS = (3, 2, 1)
 PEERS = (0, 2, 1, 3)
 ORDER = (2, 1, 3)
 HELD = 5
@@ -272,7 +273,7 @@
     )(*queries, vmem(kv), vmem(bias))
 
 
-def project_kernel(parts_ref, held, w_hbm, out_ref, sheet, w, sems):
+def project_kernel(parts_ref, held, w_hbm, keep_ref, give_ref, sheet, w, result, sems):
     wide = HD * HEAD
     copies = []
     for j in range(HELD, GROUP):
@@ -308,7 +309,7 @@
         sheet[...].astype(BF16), spread, preferred_element_type=F32
     ).astype(BF16)
     block = lax.broadcasted_iota(jnp.int32, (ROWS, wide), 1) % HEAD
-    total = jnp.zeros((HEAD * ROWS, out_ref.shape[2]), F32)
+    total = jnp.zeros((HEAD * ROWS, keep_ref.shape[2]), F32)
     for j in range(GROUP):
         if j < HELD:
             weight = held[j * wide : (j + 1) * wide, :]
@@ -320,7 +321,13 @@
             [jnp.where(block == h, rows_j, jnp.zeros_like(rows_j)) for h in range(HEAD)], axis=0
         )
         total = total + jnp.dot(lhs, weight, preferred_element_type=F32)
-    out_ref[...] = total.reshape(out_ref.shape).astype(BF16)
+    result[...] = total
+    chip, core = lax.axis_index("head") // 2, lax.axis_index("head") % 2
+    for t in range(HEAD // 2):
+        mine = ((chip ^ t) * 2 + core) * ROWS
+        other = ((chip ^ t) * 2 + 1 - core) * ROWS
+        keep_ref[t] = result[pl.ds(pl.multiple_of(mine, ROWS), ROWS), :]
+        give_ref[t] = result[pl.ds(pl.multiple_of(other, ROWS), ROWS), :].astype(BF16)
 
 
 def project(parts, held, weight):
@@ -328,11 +335,15 @@
     return pl.pallas_call(
         project_kernel,
         in_specs=[VMEM, VMEM, HBM],
-        out_specs=VMEM,
-        out_shape=pltpu.VMEM((HEAD, ROWS, cols), BF16),
+        out_specs=[VMEM, VMEM],
+        out_shape=[
+            pltpu.VMEM((HEAD // 2, ROWS, cols), F32),
+            pltpu.VMEM((HEAD // 2, ROWS, cols), BF16),
+        ],
         scratch_shapes=[
             pltpu.VMEM((GROUP * ROWS, HD), F32),
             pltpu.VMEM((GROUP - HELD, HD * HEAD, cols), BF16),
+            pltpu.VMEM((HEAD * ROWS, cols), F32),
             pltpu.SemaphoreType.DMA((GROUP - HELD,)),
         ],
         compiler_params=pltpu.CompilerParams(vmem_limit_bytes=8 * 1024 * 1024),
@@ -343,22 +354,22 @@
     )(parts, vmem(held), hbm(weight))
 
 
-def total_kernel(terms_ref, out_ref):
-    total = jnp.sum(terms_ref[...].astype(F32), axis=0)
+def total_kernel(a_ref, b_ref, c_ref, d_ref, out_ref):
+    total = sum(ref[...].astype(F32) for ref in (b_ref, c_ref, d_ref)) + a_ref[...].astype(F32)
     for s in range(STEPS):
         out_ref[s] = total[s * CACHE : (s + 1) * CACHE].astype(BF16)
 
 
 def total_of(terms):
-    cols = terms.shape[2]
+    cols = terms[0].shape[1]
     return pl.pallas_call(
         total_kernel,
-        in_specs=[VMEM],
+        in_specs=[VMEM] * 4,
         out_specs=VMEM,
         out_shape=jax.ShapeDtypeStruct((STEPS, CACHE, cols), BF16),
         compiler_params=pltpu.CompilerParams(vmem_limit_bytes=1024 * 1024),
         name="total",
-    )(terms)
+    )(*terms)
 
 
 def body(prompt_kv, kept, live_count, queries, out_weight, prefill_x, prefill_gain, kv_weight):
@@ -372,8 +383,12 @@
     sent = lax.all_to_all(parts, ("pre", "cache"), split_axis=0, concat_axis=0, tiled=True)
     weight = out_weight.reshape(8192, 256)
     next_kv, held = finish(*taken, weight, *begun, parts)
-    terms = project(sent, held, weight)
-    terms = lax.all_to_all(terms, "head", split_axis=0, concat_axis=0, tiled=True)
+    keep, give = project(sent, held, weight)
+    got = lax.ppermute(give, "head", [(i, i ^ 1) for i in range(HEAD)])
+    pairs = (keep + got.astype(F32)).astype(BF16)
+    terms = [pairs[0]]
+    for t in TURNS:
+        terms.append(lax.ppermute(pairs[t], "head", [(i, i ^ (2 * t)) for i in range(HEAD)]))
     attended = total_of(terms)
     return (attended.reshape(STEPS, CACHE, 1, 256), next_kv.reshape(512, 1, 256))
 

time: 38.2 us -> 37.2 us (0.974)
  blocking collectives: 12 us -> 0 us
  starting transfers between devices: 11.2 us -> 17.7 us
  waiting for transfers between devices: 1.07 us -> 5.27 us
    all_to_all x1 -> x0, blocking collectives: 12 us -> none  [body(): lax.all_to_all(terms, 'head', split_axis=0, concat_axis=0, tiled=True)]
    ppermute x0 -> x4, starting transfers between devices: none -> 6.44 us  [the longest x3 3.48 us: body(): lax.ppermute(pairs[t], 'head', [(i, i ^ 2 * t) for i in range(HEAD)])]
    ppermute x0 -> x4, waiting for transfers between devices: none -> 4.2 us  [the longest x3 3.34 us: body(): lax.ppermute(pairs[t], 'head', [(i, i ^ 2 * t) for i in range(HEAD)])]
  transfers between devices with their start and end apart: 4 -> 8, of which waited for: 2 -> 5; matrix products, arithmetic and copies ran while one was open for 0% -> 0% of each run, Pallas kernels for 24% -> 25%
where the time goes in v4:
time: 37.2 us; the launch traced here: 36.6 us
  starting transfers between devices  17.7 us (48%)
  Pallas kernels  12.9 us (35%)
  waiting for transfers between devices  5.27 us (14%)
  between operations  0.7 us (2%)
    all_to_all x1, starting transfers between devices, body(): lax.all_to_all(parts, ('pre', 'cache'), split_axis=0, concat_axis=0, tile...  6.72 us
    pallas_call x1, Pallas kernels, finish(): pl.pallas_call(finish_kernel, in_specs=[HBM] * 4 + [VMEM] * 2 + [ANY], ou...  6.24 us
    ppermute x3, starting transfers between devices, body(): around[k] = lax.ppermute(queries, 'pre', [(i, i ^ k) for i in range(PRE)])  4.52 us
    ppermute x3, starting transfers between devices, body(): lax.ppermute(pairs[t], 'head', [(i, i ^ 2 * t) for i in range(HEAD)])  3.48 us
    ppermute x3, waiting for transfers between devices, body(): lax.ppermute(pairs[t], 'head', [(i, i ^ 2 * t) for i in range(HEAD)])  3.34 us
    pallas_call x1, Pallas kernels, begin(): pl.pallas_call(begin_kernel, in_specs=[HBM] * 6, out_specs=[VMEM] * 4, ou...  2.96 us
    ppermute x1, starting transfers between devices, body(): got = lax.ppermute(give, 'head', [(i, i ^ 1) for i in range(HEAD)])  2.96 us
    pallas_call x1, Pallas kernels, project(): pl.pallas_call(project_kernel, in_specs=[VMEM, VMEM, HBM], out_specs=[VME...  1.7 us
  transfers between devices with their start and end apart: 8, of which 5 were waited for; matrix products, arithmetic and copies ran while one was open for 0% of the time, Pallas kernels for 25%

profile of v4, /device:TPU:1, one launch (start us, length us, event | category | flops | bytes accessed | tf_op | source)
XLA Modules:
  0.0 36.6 jit_solution(17430383627077605802)
XLA Ops:
  0.6 3.7 %collective-permute-start = (bf16[3,4,1024]{2,1,0:T(4,128)(2,1)}, bf16[3,4,1024]{2,1,0:T(4,128)(2,1)S(1)}, u32[]{:S(2)}, u32[]{:S(2)}) collective-permute-start(bf16[3,4,1024]{2,1,0:T(4,128)(2,1)} %bitcast.17), channel_id=1, source_target_pairs={{0,64},{32,96},{64,0},{96,32},{1,65},{33,97},{65,1},{97,33},{2,66}... | collective-permute-start | bytes 73736 | tf_op jit(solution)/shard_map/ppermute | solution.py:379
  4.3 0.3 collective-permute-start.1
  4.6 0.6 %collective-permute-start.2 = (bf16[3,4,1024]{2,1,0:T(4,128)(2,1)}, bf16[3,4,1024]{2,1,0:T(4,128)(2,1)S(1)}, u32[]{:S(2)}, u32[]{:S(2)}) collective-permute-start(bf16[3,4,1024]{2,1,0:T(4,128)(2,1)} %bitcast.19), channel_id=1, source_target_pairs={{0,96},{32,64},{64,32},{96,0},{1,97},{33,65},{65,33},{97,1},{2,98}... | collective-permute-start | bytes 73736 | tf_op jit(solution)/shard_map/ppermute | solution.py:379
  5.1 0.0 copy-start
  5.1 3.0 %begin.1 = (bf16[4,8,128,256]{3,2,1,0:T(8,128)(2,1)S(1)}, f32[4,1024]{1,0:T(4,128)S(1)}, f32[512,256]{1,0:T(8,128)S(1)}, f32[512,128]{1,0:T(8,128)S(1)}) custom-call(s32[4,8]{1,0:T(4,128)} %bitcast.26, s32[4]{0:T(128)} %bitcast.27, bf16[4,1,32,128,256]{4,3,2,1,0:T(8,128)(2,1)} %kv_hbm.1, bf16[512,8192]{1,0:T(8,128)(2,1)} %x_hbm.3, bf16[8192]{0:T(1024)(128)(2,1)} %gain_hbm.3, ...), custom_call_target="tpu_custom_call" | custom-call | flops 536870912 | bytes 5242880 | tf_op jit(solution)/shard_map/begin/pallas_call | solution.py:139
  8.1 0.0 collective-permute-done.q1
  8.1 0.0 collective-permute-done.1.q2
  8.1 0.6 %collective-permute-done.2.q3 = bf16[3,4,1024]{2,1,0:T(4,128)(2,1)S(1)} collective-permute-done((bf16[3,4,1024]{2,1,0:T(4,128)(2,1)}, bf16[3,4,1024]{2,1,0:T(4,128)(2,1)S(1)}, u32[]{:S(2)}, u32[]{:S(2)}) %collective-permute-start.2) | collective-permute-done | bytes 24608 | tf_op jit(solution)/shard_map/ppermute | solution.py:379
  8.7 0.0 copy-done
  8.7 1.4 %attend.1.after_ref = bf16[16,32,128]{2,1,0:T(8,128)(2,1)} custom-call(bf16[3,4,1024]{2,1,0:T(4,128)(2,1)S(1)} %bitcast.20, bf16[3,4,1024]{2,1,0:T(4,128)(2,1)S(1)} %collective-permute-done.q1, bf16[3,4,1024]{2,1,0:T(4,128)(2,1)S(1)} %collective-permute-done.1.q2, bf16[3,4,1024]{2,1,0:T(4,128)(2,1)S(1)} %collective-permute-done.2.q3, ...), custom_call_target="tpu_custom_call" | custom-call | flops 67108864 | bytes 2097152 | tf_op jit(solution)/shard_map/attend/pallas_call | solution.py:262
  10.1 6.7 %all-to-all-start = ((bf16[16,32,128]{2,1,0:T(8,128)(2,1)}), bf16[16,32,128]{2,1,0:T(8,128)(2,1)S(1)}, u32[]{:S(2)}, u32[]{:S(2)}) async-start(bf16[16,32,128]{2,1,0:T(8,128)(2,1)} %attend.1.after_ref), calls=%async_computation | async-start | bytes 262144 | tf_op jit(solution)/shard_map/all_to_all | solution.py:383
  16.8 6.2 %finish.1 = (bf16[512,256]{1,0:T(8,128)(2,1)}, bf16[5120,256]{1,0:T(8,128)(2,1)S(1)}) custom-call(bf16[512,8192]{1,0:T(8,128)(2,1)} %x_hbm.3, bf16[8192]{0:T(1024)(128)(2,1)} %gain_hbm.3, bf16[8192,256]{1,0:T(8,128)(2,1)} %bitcast.24, bf16[8192,256]{1,0:T(8,128)(2,1)} %bitcast.21, f32[512,256]{1,0:T(8,128)S(1)} %get-tuple-element.12.before, ...), custom_call_target="tpu_custom_call" | custom-call | flops 1610612736 | bytes 9437184 | tf_op jit(solution)/shard_map/finish/pallas_call | solution.py:191
  23.1 0.5 %all-to-all-done.parts_ref = bf16[16,32,128]{2,1,0:T(8,128)(2,1)S(1)} async-done(((bf16[16,32,128]{2,1,0:T(8,128)(2,1)}), bf16[16,32,128]{2,1,0:T(8,128)(2,1)S(1)}, u32[]{:S(2)}, u32[]{:S(2)}) %all-to-all-start) | async-done | bytes 131104 | tf_op jit(solution)/shard_map/all_to_all | solution.py:383
  23.6 1.7 %project.1 = (f32[4,16,256]{2,1,0:T(8,128)S(1)}, bf16[4,16,256]{2,1,0:T(8,128)(2,1)S(1)}) custom-call(bf16[16,32,128]{2,1,0:T(8,128)(2,1)S(1)} %all-to-all-done.parts_ref, bf16[5120,256]{1,0:T(8,128)(2,1)S(1)} %get-tuple-element.14.held, bf16[8192,256]{1,0:T(8,128)(2,1)} %bitcast.22), custom_call_target="tpu_custom_call" | custom-call | flops 536870912 | bytes 4194304 | tf_op jit(solution)/shard_map/project/pallas_call | solution.py:335
  25.3 3.0 %collective-permute-start.3 = (bf16[4,16,256]{2,1,0:T(8,128)(2,1)S(1)}, bf16[4,16,256]{2,1,0:T(8,128)(2,1)S(1)}, u32[]{:S(2)}, u32[]{:S(2)}) collective-permute-start(bf16[4,16,256]{2,1,0:T(8,128)(2,1)S(1)} %get-tuple-element.16), channel_id=1, source_target_pairs={{0,4},{4,0},{8,12},{12,8},{16,20},{20,16},{24,28},{28,24},{1,5},{5... | collective-permute-start | bytes 98312 | tf_op jit(solution)/shard_map/ppermute | solution.py:387
  28.3 0.9 %collective-permute-done.3 = bf16[4,16,256]{2,1,0:T(8,128)(2,1)S(1)} collective-permute-done((bf16[4,16,256]{2,1,0:T(8,128)(2,1)S(1)}, bf16[4,16,256]{2,1,0:T(8,128)(2,1)S(1)}, u32[]{:S(2)}, u32[]{:S(2)}) %collective-permute-start.3) | collective-permute-done | bytes 32800 | tf_op jit(solution)/shard_map/ppermute | solution.py:387
  29.1 2.8 %collective-permute-start.4 = (bf16[16,256]{1,0:T(8,128)(2,1)S(1)}, bf16[16,256]{1,0:T(8,128)(2,1)S(1)}, u32[]{:S(2)}, u32[]{:S(2)}) collective-permute-start(bf16[16,256]{1,0:T(8,128)(2,1)S(1)} %get-tuple-element.22), channel_id=1, source_target_pairs={{0,24},{4,28},{8,16},{12,20},{16,8},{20,12},{24,0},{28,4},{1,25},{... | collective-permute-start | bytes 24584 | tf_op jit(solution)/shard_map/ppermute | solution.py:391
  32.0 0.4 collective-permute-start.5
  32.3 0.3 collective-permute-start.6
  32.6 0.4 %collective-permute-done.4.b_ref = bf16[16,256]{1,0:T(8,128)(2,1)S(1)} collective-permute-done((bf16[16,256]{1,0:T(8,128)(2,1)S(1)}, bf16[16,256]{1,0:T(8,128)(2,1)S(1)}, u32[]{:S(2)}, u32[]{:S(2)}) %collective-permute-start.4) | collective-permute-done | bytes 8224 | tf_op jit(solution)/shard_map/ppermute | solution.py:391
  33.0 3.0 %collective-permute-done.5.c_ref = bf16[16,256]{1,0:T(8,128)(2,1)S(1)} collective-permute-done((bf16[16,256]{1,0:T(8,128)(2,1)S(1)}, bf16[16,256]{1,0:T(8,128)(2,1)S(1)}, u32[]{:S(2)}, u32[]{:S(2)}) %collective-permute-start.5) | collective-permute-done | bytes 8224 | tf_op jit(solution)/shard_map/ppermute | solution.py:391
  36.0 0.0 collective-permute-done.6.d_ref
  36.0 0.6 %total.1 = bf16[3,4,256]{2,1,0:T(4,128)(2,1)} custom-call(bf16[16,256]{1,0:T(8,128)(2,1)S(1)} %get-tuple-element.23.a_ref, bf16[16,256]{1,0:T(8,128)(2,1)S(1)} %collective-permute-done.4.b_ref, bf16[16,256]{1,0:T(8,128)(2,1)S(1)} %collective-permute-done.5.c_ref, bf16[16,256]{1,0:T(8,128)(2,1)S(1)} %collective-permute-done.6.d_ref), custom_call_target="tpu_custom_call" | custom-call | tf_op jit(solution)/shard_map/total/pallas_call | solution.py:365
  (2 shorter events, 0.0 us)
Async XLA Ops:
  0.6 7.5 %collective-permute-start = (bf16[3,4,1024]{2,1,0:T(4,128)(2,1)}, bf16[3,4,1024]{2,1,0:T(4,128)(2,1)S(1)}, u32[]{:S(2)}, u32[]{:S(2)}) collective-permute-start(bf16[3,4,1024]{2,1,0:T(4,128)(2,1)} %bitcast.17), channel_id=1, source_target_pairs={{0,64},{32,96},{64,0},{96,32},{1,65},{33,97},{65,1},{97,33},{2,66}... | collective-permute-start | bytes 73736 | tf_op jit(solution)/shard_map/ppermute | solution.py:379
  4.3 3.9 %collective-permute-start.1 = (bf16[3,4,1024]{2,1,0:T(4,128)(2,1)}, bf16[3,4,1024]{2,1,0:T(4,128)(2,1)S(1)}, u32[]{:S(2)}, u32[]{:S(2)}) collective-permute-start(bf16[3,4,1024]{2,1,0:T(4,128)(2,1)} %bitcast.18), channel_id=1, source_target_pairs={{0,32},{32,0},{64,96},{96,64},{1,33},{33,1},{65,97},{97,65},{2,34}... | collective-permute-start | bytes 73736 | tf_op jit(solution)/shard_map/ppermute | solution.py:379
  4.6 4.1 %collective-permute-start.2 = (bf16[3,4,1024]{2,1,0:T(4,128)(2,1)}, bf16[3,4,1024]{2,1,0:T(4,128)(2,1)S(1)}, u32[]{:S(2)}, u32[]{:S(2)}) collective-permute-start(bf16[3,4,1024]{2,1,0:T(4,128)(2,1)} %bitcast.19), channel_id=1, source_target_pairs={{0,96},{32,64},{64,32},{96,0},{1,97},{33,65},{65,33},{97,1},{2,98}... | collective-permute-start | bytes 73736 | tf_op jit(solution)/shard_map/ppermute | solution.py:379
  5.1 3.5 %copy-start = (bf16[3,4,1,1024]{3,1,2,0:T(4,128)(2,1)S(1)}, bf16[3,4,1,1024]{3,1,2,0:T(4,128)(2,1)}, u32[]{:S(2)}) copy-start(bf16[3,4,1,1024]{3,1,2,0:T(4,128)(2,1)} %param.11) | copy-start | bytes 73732
  10.1 13.5 %all-to-all-start = ((bf16[16,32,128]{2,1,0:T(8,128)(2,1)}), bf16[16,32,128]{2,1,0:T(8,128)(2,1)S(1)}, u32[]{:S(2)}, u32[]{:S(2)}) async-start(bf16[16,32,128]{2,1,0:T(8,128)(2,1)} %attend.1.after_ref), calls=%async_computation | async-start | bytes 262144 | tf_op jit(solution)/shard_map/all_to_all | solution.py:383
  25.3 3.8 %collective-permute-start.3 = (bf16[4,16,256]{2,1,0:T(8,128)(2,1)S(1)}, bf16[4,16,256]{2,1,0:T(8,128)(2,1)S(1)}, u32[]{:S(2)}, u32[]{:S(2)}) collective-permute-start(bf16[4,16,256]{2,1,0:T(8,128)(2,1)S(1)} %get-tuple-element.16), channel_id=1, source_target_pairs={{0,4},{4,0},{8,12},{12,8},{16,20},{20,16},{24,28},{28,24},{1,5},{5... | collective-permute-start | bytes 98312 | tf_op jit(solution)/shard_map/ppermute | solution.py:387
  29.1 3.8 %collective-permute-start.4 = (bf16[16,256]{1,0:T(8,128)(2,1)S(1)}, bf16[16,256]{1,0:T(8,128)(2,1)S(1)}, u32[]{:S(2)}, u32[]{:S(2)}) collective-permute-start(bf16[16,256]{1,0:T(8,128)(2,1)S(1)} %get-tuple-element.22), channel_id=1, source_target_pairs={{0,24},{4,28},{8,16},{12,20},{16,8},{20,12},{24,0},{28,4},{1,25},{... | collective-permute-start | bytes 24584 | tf_op jit(solution)/shard_map/ppermute | solution.py:391
  32.0 4.0 %collective-permute-start.5 = (bf16[16,256]{1,0:T(8,128)(2,1)S(1)}, bf16[16,256]{1,0:T(8,128)(2,1)S(1)}, u32[]{:S(2)}, u32[]{:S(2)}) collective-permute-start(bf16[16,256]{1,0:T(8,128)(2,1)S(1)} %get-tuple-element.21), channel_id=1, source_target_pairs={{0,16},{4,20},{8,24},{12,28},{16,0},{20,4},{24,8},{28,12},{1,17},{... | collective-permute-start | bytes 24584 | tf_op jit(solution)/shard_map/ppermute | solution.py:391
  32.3 3.7 %collective-permute-start.6 = (bf16[16,256]{1,0:T(8,128)(2,1)S(1)}, bf16[16,256]{1,0:T(8,128)(2,1)S(1)}, u32[]{:S(2)}, u32[]{:S(2)}) collective-permute-start(bf16[16,256]{1,0:T(8,128)(2,1)S(1)} %get-tuple-element.20), channel_id=1, source_target_pairs={{0,8},{4,12},{8,0},{12,4},{16,24},{20,28},{24,16},{28,20},{1,9},{5... | collective-permute-start | bytes 24584 | tf_op jit(solution)/shard_map/ppermute | solution.py:391

commit v5 on v4

--- a/solution.py
+++ b/solution.py
@@ -28,7 +28,7 @@
 AHEAD = 4
 TALL = 128
 FIRST = 2
-TURNS = (3, 2, 1)
+TURNS = ((0, 0), (2, 3), (3, 2), (1, 1))
 PEERS = (0, 2, 1, 3)
 ORDER = (2, 1, 3)
 HELD = 5
@@ -323,9 +323,9 @@
         total = total + jnp.dot(lhs, weight, preferred_element_type=F32)
     result[...] = total
     chip, core = lax.axis_index("head") // 2, lax.axis_index("head") % 2
-    for t in range(HEAD // 2):
-        mine = ((chip ^ t) * 2 + core) * ROWS
-        other = ((chip ^ t) * 2 + 1 - core) * ROWS
+    for t, (first, second) in enumerate(TURNS):
+        mine = ((chip ^ (first + (second - first) * core)) * 2 + core) * ROWS
+        other = ((chip ^ (second + (first - second) * core)) * 2 + 1 - core) * ROWS
         keep_ref[t] = result[pl.ds(pl.multiple_of(mine, ROWS), ROWS), :]
         give_ref[t] = result[pl.ds(pl.multiple_of(other, ROWS), ROWS), :].astype(BF16)
 
@@ -387,8 +387,9 @@
     got = lax.ppermute(give, "head", [(i, i ^ 1) for i in range(HEAD)])
     pairs = (keep + got.astype(F32)).astype(BF16)
     terms = [pairs[0]]
-    for t in TURNS:
-        terms.append(lax.ppermute(pairs[t], "head", [(i, i ^ (2 * t)) for i in range(HEAD)]))
+    for t in range(1, len(TURNS)):
+        moves = [(i, i ^ (2 * TURNS[t][i % 2])) for i in range(HEAD)]
+        terms.append(lax.ppermute(pairs[t], "head", moves))
     attended = total_of(terms)
     return (attended.reshape(STEPS, CACHE, 1, 256), next_kv.reshape(512, 1, 256))
 

time: 37.2 us -> 37.1 us (level)
  no operation moved by 1% of the time
where the time goes in v5:
time: 37.1 us; the launch traced here: 36.6 us
  starting transfers between devices  17.7 us (48%)
  Pallas kernels  12.9 us (35%)
  waiting for transfers between devices  5.27 us (14%)
  between operations  0.7 us (2%)
    all_to_all x1, starting transfers between devices, body(): lax.all_to_all(parts, ('pre', 'cache'), split_axis=0, concat_axis=0, tile...  6.72 us
    pallas_call x1, Pallas kernels, finish(): pl.pallas_call(finish_kernel, in_specs=[HBM] * 4 + [VMEM] * 2 + [ANY], ou...  6.24 us
    ppermute x3, starting transfers between devices, body(): around[k] = lax.ppermute(queries, 'pre', [(i, i ^ k) for i in range(PRE)])  4.52 us
    ppermute x3, starting transfers between devices, body(): terms.append(lax.ppermute(pairs[t], 'head', moves))  3.48 us
    ppermute x3, waiting for transfers between devices, body(): terms.append(lax.ppermute(pairs[t], 'head', moves))  3.34 us
    pallas_call x1, Pallas kernels, begin(): pl.pallas_call(begin_kernel, in_specs=[HBM] * 6, out_specs=[VMEM] * 4, ou...  2.96 us
    ppermute x1, starting transfers between devices, body(): got = lax.ppermute(give, 'head', [(i, i ^ 1) for i in range(HEAD)])  2.96 us
    pallas_call x1, Pallas kernels, project(): pl.pallas_call(project_kernel, in_specs=[VMEM, VMEM, HBM], out_specs=[VME...  1.7 us
  transfers between devices with their start and end apart: 8, of which 5 were waited for; matrix products, arithmetic and copies ran while one was open for 0% of the time, Pallas kernels for 25%

profile of v5, /device:TPU:1, one launch (start us, length us, event | category | flops | bytes accessed | tf_op | source)
XLA Modules:
  0.0 36.6 jit_solution(5065813439953498905)
XLA Ops:
  0.6 3.7 %collective-permute-start = (bf16[3,4,1024]{2,1,0:T(4,128)(2,1)}, bf16[3,4,1024]{2,1,0:T(4,128)(2,1)S(1)}, u32[]{:S(2)}, u32[]{:S(2)}) collective-permute-start(bf16[3,4,1024]{2,1,0:T(4,128)(2,1)} %bitcast.17), channel_id=1, source_target_pairs={{0,64},{32,96},{64,0},{96,32},{1,65},{33,97},{65,1},{97,33},{2,66}... | collective-permute-start | bytes 73736 | tf_op jit(solution)/shard_map/ppermute | solution.py:379
  4.3 0.3 collective-permute-start.1
  4.6 0.6 %collective-permute-start.2 = (bf16[3,4,1024]{2,1,0:T(4,128)(2,1)}, bf16[3,4,1024]{2,1,0:T(4,128)(2,1)S(1)}, u32[]{:S(2)}, u32[]{:S(2)}) collective-permute-start(bf16[3,4,1024]{2,1,0:T(4,128)(2,1)} %bitcast.19), channel_id=1, source_target_pairs={{0,96},{32,64},{64,32},{96,0},{1,97},{33,65},{65,33},{97,1},{2,98}... | collective-permute-start | bytes 73736 | tf_op jit(solution)/shard_map/ppermute | solution.py:379
  5.1 0.0 copy-start
  5.1 3.0 %begin.1 = (bf16[4,8,128,256]{3,2,1,0:T(8,128)(2,1)S(1)}, f32[4,1024]{1,0:T(4,128)S(1)}, f32[512,256]{1,0:T(8,128)S(1)}, f32[512,128]{1,0:T(8,128)S(1)}) custom-call(s32[4,8]{1,0:T(4,128)} %bitcast.26, s32[4]{0:T(128)} %bitcast.27, bf16[4,1,32,128,256]{4,3,2,1,0:T(8,128)(2,1)} %kv_hbm.1, bf16[512,8192]{1,0:T(8,128)(2,1)} %x_hbm.3, bf16[8192]{0:T(1024)(128)(2,1)} %gain_hbm.3, ...), custom_call_target="tpu_custom_call" | custom-call | flops 536870912 | bytes 5242880 | tf_op jit(solution)/shard_map/begin/pallas_call | solution.py:139
  8.1 0.0 collective-permute-done.q1
  8.1 0.0 collective-permute-done.1.q2
  8.1 0.6 %collective-permute-done.2.q3 = bf16[3,4,1024]{2,1,0:T(4,128)(2,1)S(1)} collective-permute-done((bf16[3,4,1024]{2,1,0:T(4,128)(2,1)}, bf16[3,4,1024]{2,1,0:T(4,128)(2,1)S(1)}, u32[]{:S(2)}, u32[]{:S(2)}) %collective-permute-start.2) | collective-permute-done | bytes 24608 | tf_op jit(solution)/shard_map/ppermute | solution.py:379
  8.7 0.0 copy-done
  8.7 1.4 %attend.1.after_ref = bf16[16,32,128]{2,1,0:T(8,128)(2,1)} custom-call(bf16[3,4,1024]{2,1,0:T(4,128)(2,1)S(1)} %bitcast.20, bf16[3,4,1024]{2,1,0:T(4,128)(2,1)S(1)} %collective-permute-done.q1, bf16[3,4,1024]{2,1,0:T(4,128)(2,1)S(1)} %collective-permute-done.1.q2, bf16[3,4,1024]{2,1,0:T(4,128)(2,1)S(1)} %collective-permute-done.2.q3, ...), custom_call_target="tpu_custom_call" | custom-call | flops 67108864 | bytes 2097152 | tf_op jit(solution)/shard_map/attend/pallas_call | solution.py:262
  10.1 6.7 %all-to-all-start = ((bf16[16,32,128]{2,1,0:T(8,128)(2,1)}), bf16[16,32,128]{2,1,0:T(8,128)(2,1)S(1)}, u32[]{:S(2)}, u32[]{:S(2)}) async-start(bf16[16,32,128]{2,1,0:T(8,128)(2,1)} %attend.1.after_ref), calls=%async_computation | async-start | bytes 262144 | tf_op jit(solution)/shard_map/all_to_all | solution.py:383
  16.8 6.2 %finish.1 = (bf16[512,256]{1,0:T(8,128)(2,1)}, bf16[5120,256]{1,0:T(8,128)(2,1)S(1)}) custom-call(bf16[512,8192]{1,0:T(8,128)(2,1)} %x_hbm.3, bf16[8192]{0:T(1024)(128)(2,1)} %gain_hbm.3, bf16[8192,256]{1,0:T(8,128)(2,1)} %bitcast.24, bf16[8192,256]{1,0:T(8,128)(2,1)} %bitcast.21, f32[512,256]{1,0:T(8,128)S(1)} %get-tuple-element.12.before, ...), custom_call_target="tpu_custom_call" | custom-call | flops 1610612736 | bytes 9437184 | tf_op jit(solution)/shard_map/finish/pallas_call | solution.py:191
  23.1 0.5 %all-to-all-done.parts_ref = bf16[16,32,128]{2,1,0:T(8,128)(2,1)S(1)} async-done(((bf16[16,32,128]{2,1,0:T(8,128)(2,1)}), bf16[16,32,128]{2,1,0:T(8,128)(2,1)S(1)}, u32[]{:S(2)}, u32[]{:S(2)}) %all-to-all-start) | async-done | bytes 131104 | tf_op jit(solution)/shard_map/all_to_all | solution.py:383
  23.6 1.7 %project.1 = (f32[4,16,256]{2,1,0:T(8,128)S(1)}, bf16[4,16,256]{2,1,0:T(8,128)(2,1)S(1)}) custom-call(bf16[16,32,128]{2,1,0:T(8,128)(2,1)S(1)} %all-to-all-done.parts_ref, bf16[5120,256]{1,0:T(8,128)(2,1)S(1)} %get-tuple-element.14.held, bf16[8192,256]{1,0:T(8,128)(2,1)} %bitcast.22), custom_call_target="tpu_custom_call" | custom-call | flops 536870912 | bytes 4194304 | tf_op jit(solution)/shard_map/project/pallas_call | solution.py:335
  25.3 3.0 %collective-permute-start.3 = (bf16[4,16,256]{2,1,0:T(8,128)(2,1)S(1)}, bf16[4,16,256]{2,1,0:T(8,128)(2,1)S(1)}, u32[]{:S(2)}, u32[]{:S(2)}) collective-permute-start(bf16[4,16,256]{2,1,0:T(8,128)(2,1)S(1)} %get-tuple-element.16), channel_id=1, source_target_pairs={{0,4},{4,0},{8,12},{12,8},{16,20},{20,16},{24,28},{28,24},{1,5},{5... | collective-permute-start | bytes 98312 | tf_op jit(solution)/shard_map/ppermute | solution.py:387
  28.3 0.9 %collective-permute-done.3 = bf16[4,16,256]{2,1,0:T(8,128)(2,1)S(1)} collective-permute-done((bf16[4,16,256]{2,1,0:T(8,128)(2,1)S(1)}, bf16[4,16,256]{2,1,0:T(8,128)(2,1)S(1)}, u32[]{:S(2)}, u32[]{:S(2)}) %collective-permute-start.3) | collective-permute-done | bytes 32800 | tf_op jit(solution)/shard_map/ppermute | solution.py:387
  29.2 2.8 %collective-permute-start.4 = (bf16[16,256]{1,0:T(8,128)(2,1)S(1)}, bf16[16,256]{1,0:T(8,128)(2,1)S(1)}, u32[]{:S(2)}, u32[]{:S(2)}) collective-permute-start(bf16[16,256]{1,0:T(8,128)(2,1)S(1)} %get-tuple-element.22), channel_id=1, source_target_pairs={{0,16},{4,28},{8,24},{12,20},{16,0},{20,12},{24,8},{28,4},{1,17},{... | collective-permute-start | bytes 24584 | tf_op jit(solution)/shard_map/ppermute | solution.py:392
  32.0 0.4 collective-permute-start.5
  32.3 0.3 collective-permute-start.6
  32.6 0.4 %collective-permute-done.4.b_ref = bf16[16,256]{1,0:T(8,128)(2,1)S(1)} collective-permute-done((bf16[16,256]{1,0:T(8,128)(2,1)S(1)}, bf16[16,256]{1,0:T(8,128)(2,1)S(1)}, u32[]{:S(2)}, u32[]{:S(2)}) %collective-permute-start.4) | collective-permute-done | bytes 8224 | tf_op jit(solution)/shard_map/ppermute | solution.py:392
  33.0 3.0 %collective-permute-done.5.c_ref = bf16[16,256]{1,0:T(8,128)(2,1)S(1)} collective-permute-done((bf16[16,256]{1,0:T(8,128)(2,1)S(1)}, bf16[16,256]{1,0:T(8,128)(2,1)S(1)}, u32[]{:S(2)}, u32[]{:S(2)}) %collective-permute-start.5) | collective-permute-done | bytes 8224 | tf_op jit(solution)/shard_map/ppermute | solution.py:392
  36.0 0.0 collective-permute-done.6.d_ref
  36.0 0.6 %total.1 = bf16[3,4,256]{2,1,0:T(4,128)(2,1)} custom-call(bf16[16,256]{1,0:T(8,128)(2,1)S(1)} %get-tuple-element.23.a_ref, bf16[16,256]{1,0:T(8,128)(2,1)S(1)} %collective-permute-done.4.b_ref, bf16[16,256]{1,0:T(8,128)(2,1)S(1)} %collective-permute-done.5.c_ref, bf16[16,256]{1,0:T(8,128)(2,1)S(1)} %collective-permute-done.6.d_ref), custom_call_target="tpu_custom_call" | custom-call | tf_op jit(solution)/shard_map/total/pallas_call | solution.py:365
  (2 shorter events, 0.0 us)
Async XLA Ops:
  0.6 7.5 %collective-permute-start = (bf16[3,4,1024]{2,1,0:T(4,128)(2,1)}, bf16[3,4,1024]{2,1,0:T(4,128)(2,1)S(1)}, u32[]{:S(2)}, u32[]{:S(2)}) collective-permute-start(bf16[3,4,1024]{2,1,0:T(4,128)(2,1)} %bitcast.17), channel_id=1, source_target_pairs={{0,64},{32,96},{64,0},{96,32},{1,65},{33,97},{65,1},{97,33},{2,66}... | collective-permute-start | bytes 73736 | tf_op jit(solution)/shard_map/ppermute | solution.py:379
  4.3 3.9 %collective-permute-start.1 = (bf16[3,4,1024]{2,1,0:T(4,128)(2,1)}, bf16[3,4,1024]{2,1,0:T(4,128)(2,1)S(1)}, u32[]{:S(2)}, u32[]{:S(2)}) collective-permute-start(bf16[3,4,1024]{2,1,0:T(4,128)(2,1)} %bitcast.18), channel_id=1, source_target_pairs={{0,32},{32,0},{64,96},{96,64},{1,33},{33,1},{65,97},{97,65},{2,34}... | collective-permute-start | bytes 73736 | tf_op jit(solution)/shard_map/ppermute | solution.py:379
  4.6 4.1 %collective-permute-start.2 = (bf16[3,4,1024]{2,1,0:T(4,128)(2,1)}, bf16[3,4,1024]{2,1,0:T(4,128)(2,1)S(1)}, u32[]{:S(2)}, u32[]{:S(2)}) collective-permute-start(bf16[3,4,1024]{2,1,0:T(4,128)(2,1)} %bitcast.19), channel_id=1, source_target_pairs={{0,96},{32,64},{64,32},{96,0},{1,97},{33,65},{65,33},{97,1},{2,98}... | collective-permute-start | bytes 73736 | tf_op jit(solution)/shard_map/ppermute | solution.py:379
  5.1 3.5 %copy-start = (bf16[3,4,1,1024]{3,1,2,0:T(4,128)(2,1)S(1)}, bf16[3,4,1,1024]{3,1,2,0:T(4,128)(2,1)}, u32[]{:S(2)}) copy-start(bf16[3,4,1,1024]{3,1,2,0:T(4,128)(2,1)} %param.11) | copy-start | bytes 73732
  10.1 13.5 %all-to-all-start = ((bf16[16,32,128]{2,1,0:T(8,128)(2,1)}), bf16[16,32,128]{2,1,0:T(8,128)(2,1)S(1)}, u32[]{:S(2)}, u32[]{:S(2)}) async-start(bf16[16,32,128]{2,1,0:T(8,128)(2,1)} %attend.1.after_ref), calls=%async_computation | async-start | bytes 262144 | tf_op jit(solution)/shard_map/all_to_all | solution.py:383
  25.3 3.8 %collective-permute-start.3 = (bf16[4,16,256]{2,1,0:T(8,128)(2,1)S(1)}, bf16[4,16,256]{2,1,0:T(8,128)(2,1)S(1)}, u32[]{:S(2)}, u32[]{:S(2)}) collective-permute-start(bf16[4,16,256]{2,1,0:T(8,128)(2,1)S(1)} %get-tuple-element.16), channel_id=1, source_target_pairs={{0,4},{4,0},{8,12},{12,8},{16,20},{20,16},{24,28},{28,24},{1,5},{5... | collective-permute-start | bytes 98312 | tf_op jit(solution)/shard_map/ppermute | solution.py:387
  29.2 3.8 %collective-permute-start.4 = (bf16[16,256]{1,0:T(8,128)(2,1)S(1)}, bf16[16,256]{1,0:T(8,128)(2,1)S(1)}, u32[]{:S(2)}, u32[]{:S(2)}) collective-permute-start(bf16[16,256]{1,0:T(8,128)(2,1)S(1)} %get-tuple-element.22), channel_id=1, source_target_pairs={{0,16},{4,28},{8,24},{12,20},{16,0},{20,12},{24,8},{28,4},{1,17},{... | collective-permute-start | bytes 24584 | tf_op jit(solution)/shard_map/ppermute | solution.py:392
  32.0 4.0 %collective-permute-start.5 = (bf16[16,256]{1,0:T(8,128)(2,1)S(1)}, bf16[16,256]{1,0:T(8,128)(2,1)S(1)}, u32[]{:S(2)}, u32[]{:S(2)}) collective-permute-start(bf16[16,256]{1,0:T(8,128)(2,1)S(1)} %get-tuple-element.21), channel_id=1, source_target_pairs={{0,24},{4,20},{8,16},{12,28},{16,8},{20,4},{24,0},{28,12},{1,25},{... | collective-permute-start | bytes 24584 | tf_op jit(solution)/shard_map/ppermute | solution.py:392
  32.3 3.7 %collective-permute-start.6 = (bf16[16,256]{1,0:T(8,128)(2,1)S(1)}, bf16[16,256]{1,0:T(8,128)(2,1)S(1)}, u32[]{:S(2)}, u32[]{:S(2)}) collective-permute-start(bf16[16,256]{1,0:T(8,128)(2,1)S(1)} %get-tuple-element.20), channel_id=1, source_target_pairs={{0,8},{4,12},{8,0},{12,4},{16,24},{20,28},{24,16},{28,20},{1,9},{5... | collective-permute-start | bytes 24584 | tf_op jit(solution)/shard_map/ppermute | solution.py:392
